TPU v7x, 512 devices: a whole 4x8x8 slice. The times are simulated.
512 devices in a mesh: dp: 4 (over y_lo), seq: 32 (over z, x), head: 4 (over y_hi, core).
Axes of the slice: x: 4, y: 8 (y_hi: 2, y_lo: 4; y = y_hi * 4 + y_lo), z: 8, core: 2. Of those that a mesh axis runs over, the one named last changes fastest.
Arguments:
- queries: bfloat16 [28672, 1024], P(('dp', 'seq', 'head')), parts along dimension 0, may hold values from -6 to 6
- key_rows: bfloat16 [28672, 1024], P(('dp', 'seq', 'head')), parts along dimension 0, may hold values from -6 to 6
- values: bfloat16 [28672, 1024], P(('dp', 'seq', 'head')), parts along dimension 0, may hold values from -6 to 6
- query_tangent: bfloat16 [28672, 1024], P(('dp', 'seq', 'head')), parts along dimension 0, may hold values from -6 to 6
- key_tangent: bfloat16 [28672, 1024], P(('dp', 'seq', 'head')), parts along dimension 0, may hold values from -6 to 6
- value_tangent: bfloat16 [28672, 1024], P(('dp', 'seq', 'head')), parts along dimension 0, may hold values from -6 to 6
- out_weight: bfloat16 [1024, 1536], replicated, may hold values from -4 to 4
- gate_vector: float32 [6144], P('dp'), parts along dimension 0, may hold values from 0.1 to 1.9
- gate_tangent: float32 [6144], P('dp'), parts along dimension 0, may hold values from -6 to 6
Outputs:
- block_out: bfloat16 [28672, 1536], P(('dp', 'seq', 'head')), parts along dimension 0
- block_tangent: bfloat16 [28672, 1536], P(('dp', 'seq', 'head')), parts along dimension 0
There are 4 independent parts, one for each index of `dp`. A program takes and returns all parts, laid end to end along the dimension named above; an argument that names none is the same for every part. Nothing has to cross between parts.
All inputs are finite; a program needn't handle non-finite values.
Results may differ from a plain program's by a relative error of at most 0.014.
Values may be sent and summed in bfloat16 or wider, within the bound.
A program may use at most 64 MiB of HBM per device.

v0:
```python
import jax
import jax.numpy as jnp
from jax import lax
from jax.sharding import PartitionSpec as P

HD = 128


def local(
    queries,
    key_rows,
    values,
    query_tangent,
    key_tangent,
    value_tangent,
    out_weight,
    gate_vector,
    gate_tangent,
):
    queries, key_rows, values, query_tangent, key_tangent, value_tangent = (
        lax.all_to_all(queries, "head", split_axis=1, concat_axis=0, tiled=True),
        lax.all_to_all(key_rows, "head", split_axis=1, concat_axis=0, tiled=True),
        lax.all_to_all(values, "head", split_axis=1, concat_axis=0, tiled=True),
        lax.all_to_all(query_tangent, "head", split_axis=1, concat_axis=0, tiled=True),
        lax.all_to_all(key_tangent, "head", split_axis=1, concat_axis=0, tiled=True),
        lax.all_to_all(value_tangent, "head", split_axis=1, concat_axis=0, tiled=True),
    )
    row_count = queries.shape[0]
    col_width = queries.shape[1]
    heads_here = col_width // HD
    score_scale = HD ** (-0.5)

    def by_head(matrix):
        return matrix.reshape(matrix.shape[0], heads_here, HD)

    query_heads = by_head(queries)
    query_dots = by_head(query_tangent)

    def absorb(state_now, block):
        key_head, value_head, key_dot, value_dot = tuple((by_head(member) for member in block))
        row_max, row_total, tilt_sum, weighted, tangent_acc = state_now
        scores = (
            jnp.einsum("qhd,khd->hqk", query_heads, key_head, preferred_element_type=jnp.float32)
            * score_scale
        )
        score_tangent = (
            jnp.einsum("qhd,khd->hqk", query_dots, key_head, preferred_element_type=jnp.float32)
            + jnp.einsum("qhd,khd->hqk", query_heads, key_dot, preferred_element_type=jnp.float32)
        ) * score_scale
        new_max = jnp.maximum(row_max, jnp.max(scores, axis=-1))
        rescale = jnp.exp(row_max - new_max)
        weights = jnp.exp(scores - new_max[:, :, None]).astype(jnp.bfloat16)
        weight_wide = weights.astype(jnp.float32)
        shifted = weight_wide * score_tangent
        row_total = row_total * rescale + jnp.sum(weight_wide, axis=-1)
        tilt_sum = tilt_sum * rescale + jnp.sum(shifted, axis=-1)
        shaded = shifted.astype(jnp.bfloat16)
        rescale_rows = rescale.T[:, :, None]
        weighted = weighted * rescale_rows + jnp.einsum(
            "hqk,khd->qhd", weights, value_head, preferred_element_type=jnp.float32
        )
        tangent_acc = (
            tangent_acc * rescale_rows
            + jnp.einsum("hqk,khd->qhd", weights, value_dot, preferred_element_type=jnp.float32)
            + jnp.einsum("hqk,khd->qhd", shaded, value_head, preferred_element_type=jnp.float32)
        )
        return (new_max, row_total, tilt_sum, weighted, tangent_acc)

    start_state = (
        jnp.full((heads_here, row_count), -jnp.inf, jnp.float32),
        jnp.zeros((heads_here, row_count), jnp.float32),
        jnp.zeros((heads_here, row_count), jnp.float32),
        jnp.zeros((row_count, heads_here, HD), jnp.float32),
        jnp.zeros((row_count, heads_here, HD), jnp.float32),
    )
    key_piece = (
        lax.all_gather(key_rows, "seq", axis=0, tiled=True),
        lax.all_gather(values, "seq", axis=0, tiled=True),
        lax.all_gather(key_tangent, "seq", axis=0, tiled=True),
        lax.all_gather(value_tangent, "seq", axis=0, tiled=True),
    )
    span_rows = key_piece[0].shape[0]
    group_size = 4
    block_rows = group_size * row_count
    stacked = tuple(
        (
            member.reshape(span_rows // block_rows, block_rows, member.shape[1])
            for member in key_piece
        )
    )

    def one_block(state_in, block):
        return (absorb(state_in, block), None)

    final_state, ignored = lax.scan(one_block, start_state, stacked)
    row_max, row_total, tilt_sum, weighted, tangent_acc = final_state
    total_rows = row_total.T[:, :, None]
    attended = weighted / total_rows
    attended_tangent = tangent_acc / total_rows - tilt_sum.T[:, :, None] / total_rows * attended
    attended = attended.reshape(row_count, col_width).astype(jnp.bfloat16)
    attended_tangent = attended_tangent.reshape(row_count, col_width).astype(jnp.bfloat16)
    token_primal, token_tangent = (
        lax.all_to_all(attended, "head", split_axis=0, concat_axis=1, tiled=True),
        lax.all_to_all(attended_tangent, "head", split_axis=0, concat_axis=1, tiled=True),
    )
    projected = jnp.dot(token_primal, out_weight, preferred_element_type=jnp.float32)
    projected_tangent = jnp.dot(token_tangent, out_weight, preferred_element_type=jnp.float32)
    block_out = (gate_vector * projected).astype(jnp.bfloat16)
    block_tangent = (gate_tangent * projected + gate_vector * projected_tangent).astype(
        jnp.bfloat16
    )
    return (block_out, block_tangent)


def solution(mesh):
    placed = (
        P(("dp", "seq", "head"), None),
        P(("dp", "seq", "head"), None),
        P(("dp", "seq", "head"), None),
        P(("dp", "seq", "head"), None),
        P(("dp", "seq", "head"), None),
        P(("dp", "seq", "head"), None),
        P(),
        P("dp"),
        P("dp"),
    )
    return jax.shard_map(
        local,
        mesh=mesh,
        in_specs=placed,
        out_specs=(P(("dp", "seq", "head"), None), P(("dp", "seq", "head"), None)),
        check_vma=False,
    )
```

profile of v0, /device:TPU:1, one launch (start us, length us, event | category | flops | bytes accessed | tf_op | source)
XLA Modules:
  0.0 631.3 jit_solution(12862944125506694530)
XLA Ops:
  8.3 17.4 %all_to_all.140 = bf16[56,4,256]{2,0,1:T(8,128)(2,1)} all-to-all(bf16[56,4,256]{2,0,1:T(8,128)(2,1)S(1)} %bitcast.156), channel_id=1, replica_groups=mesh['dp'=4,'seq'=32,'head'=4] {'head'}, dimensions={1} | all-to-all | bytes 229376 | tf_op jit(solution)/shard_map/all_to_all | solution.py:23
  26.7 11.4 %all_to_all.141 = bf16[56,4,256]{2,0,1:T(8,128)(2,1)} all-to-all(bf16[56,4,256]{2,0,1:T(8,128)(2,1)S(1)} %bitcast.157), channel_id=1, replica_groups=mesh['dp'=4,'seq'=32,'head'=4] {'head'}, dimensions={1} | all-to-all | bytes 229376 | tf_op jit(solution)/shard_map/all_to_all | solution.py:26
  39.1 11.4 %all_to_all.142 = bf16[56,4,256]{2,0,1:T(8,128)(2,1)} all-to-all(bf16[56,4,256]{2,0,1:T(8,128)(2,1)S(1)} %bitcast.158), channel_id=1, replica_groups=mesh['dp'=4,'seq'=32,'head'=4] {'head'}, dimensions={1} | all-to-all | bytes 229376 | tf_op jit(solution)/shard_map/all_to_all | solution.py:22
  50.6 11.4 %all_to_all.143 = bf16[56,4,256]{2,0,1:T(8,128)(2,1)} all-to-all(bf16[56,4,256]{2,0,1:T(8,128)(2,1)S(1)} %bitcast.159), channel_id=1, replica_groups=mesh['dp'=4,'seq'=32,'head'=4] {'head'}, dimensions={1} | all-to-all | bytes 229376 | tf_op jit(solution)/shard_map/all_to_all | solution.py:25
  62.7 4.3 all-to-all-start.1
  67.6 6.7 %all-to-all-done.1 = bf16[56,4,256]{2,0,1:T(8,128)(2,1)S(1)} async-done(((bf16[56,4,256]{2,0,1:T(8,128)(2,1)}), bf16[56,4,256]{2,0,1:T(8,128)(2,1)S(1)}, u32[]{:S(2)}, u32[]{:S(2)}) %all-to-all-start.1) | async-done | bytes 114720 | tf_op jit(solution)/shard_map/all_to_all | solution.py:21
  74.3 4.3 all-to-all-start.2
  80.2 5.8 all-to-all-done.2
  87.6 21.7 %all-gather.9.cloned.1.call-done = bf16[7168,256]{1,0:T(8,128)(2,1)} async-done(((bf16[224,256]{1,0:T(8,128)(2,1)}), bf16[7168,256]{1,0:T(8,128)(2,1)}) %all-gather.9.cloned.1.call-update) | async-done | bytes 3670032 | tf_op jit(solution)/shard_map/all_gather | solution.py:78
  109.3 86.7 %all-gather.11.cloned.1.call-done = bf16[7168,256]{1,0:T(8,128)(2,1)} async-done(((bf16[224,256]{1,0:T(8,128)(2,1)}), bf16[7168,256]{1,0:T(8,128)(2,1)}) %all-gather.11.cloned.1.call-update) | async-done | bytes 3670032 | tf_op jit(solution)/shard_map/all_gather | solution.py:80
  195.9 86.7 %all-gather.5.cloned.1.call-done = bf16[7168,256]{1,0:T(8,128)(2,1)} async-done(((bf16[224,256]{1,0:T(8,128)(2,1)}), bf16[7168,256]{1,0:T(8,128)(2,1)}) %all-gather.5.cloned.1.call-update) | async-done | bytes 3670032 | tf_op jit(solution)/shard_map/all_gather | solution.py:77
  282.6 86.5 %all-gather.7.cloned.1.call-done = bf16[7168,256]{1,0:T(8,128)(2,1)} async-done(((bf16[224,256]{1,0:T(8,128)(2,1)}), bf16[7168,256]{1,0:T(8,128)(2,1)}) %all-gather.7.cloned.1.call-update) | async-done | bytes 3670032 | tf_op jit(solution)/shard_map/all_gather | solution.py:79
  369.1 221.1 %while.19 = (s32[]{:T(128)}, f32[2,224]{1,0:T(2,128)S(1)}, f32[2,224]{1,0:T(2,128)S(1)}, f32[2,224]{1,0:T(2,128)S(1)}, f32[224,2,128]{2,0,1:T(8,128)}, /*index=5...) while((s32[]{:T(128)}, f32[2,224]{1,0:T(2,128)S(1)}, ...), condition=%wide.region_4.5_spmd.clone, body=%wide.region_0.4_spmd.clone.sunk | while | flops 622185984 | bytes 32722268 | solution.py:95
  369.1 2.2 constant_dynamic-slice_fusion.6
  373.4 2.5 bitcast_reduce_fusion.2
  376.0 2.7 convert_reduce_fusion.2
  382.2 3.1 fusion.65
  385.3 2.1 constant_dynamic-slice_fusion.7
  393.1 2.5 fusion.68
  396.7 2.2 constant_dynamic-slice_fusion.6
  401.0 2.5 bitcast_reduce_fusion.2
  403.5 2.7 convert_reduce_fusion.2
  409.8 3.1 fusion.65
  412.9 2.1 constant_dynamic-slice_fusion.7
  420.7 2.5 fusion.68
  424.4 2.2 constant_dynamic-slice_fusion.6
  428.6 2.5 bitcast_reduce_fusion.2
  431.2 2.7 convert_reduce_fusion.2
  437.5 3.1 fusion.65
  440.5 2.1 constant_dynamic-slice_fusion.7
  448.4 2.5 fusion.68
  452.0 2.2 constant_dynamic-slice_fusion.6
  456.3 2.5 bitcast_reduce_fusion.2
  458.8 2.7 convert_reduce_fusion.2
  465.1 3.1 fusion.65
  468.2 2.1 constant_dynamic-slice_fusion.7
  476.0 2.5 fusion.68
  479.7 2.2 constant_dynamic-slice_fusion.6
  483.9 2.5 bitcast_reduce_fusion.2
  486.5 2.7 convert_reduce_fusion.2
  492.8 3.1 fusion.65
  495.9 2.1 constant_dynamic-slice_fusion.7
  503.7 2.5 fusion.68
  507.3 2.2 constant_dynamic-slice_fusion.6
  511.6 2.5 bitcast_reduce_fusion.2
  514.1 2.7 convert_reduce_fusion.2
  520.4 3.1 fusion.65
  523.5 2.1 constant_dynamic-slice_fusion.7
  531.3 2.5 fusion.68
  535.0 2.2 constant_dynamic-slice_fusion.6
  539.2 2.5 bitcast_reduce_fusion.2
  541.8 2.7 convert_reduce_fusion.2
  548.1 3.1 fusion.65
  551.2 2.1 constant_dynamic-slice_fusion.7
  559.0 2.5 fusion.68
  562.6 2.2 constant_dynamic-slice_fusion.6
  566.9 2.5 bitcast_reduce_fusion.2
  569.4 2.7 convert_reduce_fusion.2
  575.7 3.1 fusion.65
  586.6 2.5 fusion.68
  592.4 10.7 %all-to-all-start.6 = ((bf16[4,56,256]{2,1,0:T(8,128)(2,1)}), bf16[4,56,256]{2,1,0:T(8,128)(2,1)S(1)}, u32[]{:S(2)}, u32[]{:S(2)}) async-start(bf16[4,56,256]{2,1,0:T(8,128)(2,1)} %convert_element_type.30), calls=%async_computation.6 | async-start | bytes 229376 | tf_op jit(solution)/shard_map/all_to_all | solution.py:103
  603.9 6.6 %all-to-all-done.6 = bf16[4,56,256]{2,1,0:T(8,128)(2,1)S(1)} async-done(((bf16[4,56,256]{2,1,0:T(8,128)(2,1)}), bf16[4,56,256]{2,1,0:T(8,128)(2,1)S(1)}, u32[]{:S(2)}, u32[]{:S(2)}) %all-to-all-start.6) | async-done | bytes 114720 | tf_op jit(solution)/shard_map/all_to_all | solution.py:103
  610.4 4.3 all-to-all-start.7
  614.7 7.4 %all-to-all-done.7 = bf16[4,56,256]{2,1,0:T(8,128)(2,1)S(1)} async-done(((bf16[4,56,256]{2,1,0:T(8,128)(2,1)}), bf16[4,56,256]{2,1,0:T(8,128)(2,1)S(1)}, u32[]{:S(2)}, u32[]{:S(2)}) %all-to-all-start.7) | async-done | bytes 114720 | tf_op jit(solution)/shard_map/all_to_all | solution.py:104
  (238 shorter events, 113.9 us)
Async XLA Ops:
  7.2 614.9 %copy-start = (bf16[1024,1536]{1,0:T(8,128)(2,1)S(1)}, bf16[1024,1536]{1,0:T(8,128)(2,1)}, u32[]{:S(2)}) copy-start(bf16[1024,1536]{1,0:T(8,128)(2,1)} %param.17) | copy-start | bytes 9437188
  7.2 43.4 %copy-start.8 = (bf16[56,1024]{1,0:T(8,128)(2,1)S(1)}, bf16[56,1024]{1,0:T(8,128)(2,1)}, u32[]{:S(2)}) copy-start(bf16[56,1024]{1,0:T(8,128)(2,1)} %param.15) | copy-start | bytes 344068
  7.2 54.8 %copy-start.9 = (bf16[56,1024]{1,0:T(8,128)(2,1)S(1)}, bf16[56,1024]{1,0:T(8,128)(2,1)}, u32[]{:S(2)}) copy-start(bf16[56,1024]{1,0:T(8,128)(2,1)} %param.11) | copy-start | bytes 344068
  7.2 59.8 %copy-start.10 = (bf16[56,1024]{1,0:T(8,128)(2,1)S(1)}, bf16[56,1024]{1,0:T(8,128)(2,1)}, u32[]{:S(2)}) copy-start(bf16[56,1024]{1,0:T(8,128)(2,1)} %param.14) | copy-start | bytes 344068
  7.2 102.1 %all-gather.9.cloned.1.call-start = ((), (), s32[]{:S(2)}) async-start(), calls=%async_computation.10 | async-start | bytes 3784704 | tf_op jit(solution)/shard_map/all_gather | solution.py:78
  25.7 170.2 %all-gather.11.cloned.1.call-start = ((), (), s32[]{:S(2)}) async-start(), calls=%async_computation.11 | async-start | bytes 3784704 | tf_op jit(solution)/shard_map/all_gather | solution.py:80
  38.1 244.5 %all-gather.5.cloned.1.call-start = ((), (), s32[]{:S(2)}) async-start(), calls=%async_computation.8 | async-start | bytes 3784704 | tf_op jit(solution)/shard_map/all_gather | solution.py:77
  50.5 318.6 %all-gather.7.cloned.1.call-start = ((), (), s32[]{:S(2)}) async-start(), calls=%async_computation.9 | async-start | bytes 3784704 | tf_op jit(solution)/shard_map/all_gather | solution.py:79
  62.7 11.7 %all-to-all-start.1 = ((bf16[56,4,256]{2,0,1:T(8,128)(2,1)}), bf16[56,4,256]{2,0,1:T(8,128)(2,1)S(1)}, u32[]{:S(2)}, u32[]{:S(2)}) async-start(bf16[56,4,256]{2,0,1:T(8,128)(2,1)} %bitcast.94), calls=%async_computation.1 | async-start | bytes 229376 | tf_op jit(solution)/shard_map/all_to_all | solution.py:21
  74.3 11.7 %all-to-all-start.2 = ((bf16[56,4,256]{2,0,1:T(8,128)(2,1)}), bf16[56,4,256]{2,0,1:T(8,128)(2,1)S(1)}, u32[]{:S(2)}, u32[]{:S(2)}) async-start(bf16[56,4,256]{2,0,1:T(8,128)(2,1)} %bitcast.93), calls=%async_computation.2 | async-start | bytes 229376 | tf_op jit(solution)/shard_map/all_to_all | solution.py:24
  369.1 9.6 %copy-start.6 = (bf16[224,2,128]{2,0,1:T(8,128)(2,1)}, bf16[224,2,128]{2,0,1:T(8,128)(2,1)S(1)}, u32[]{:S(2)}) copy-start(bf16[224,2,128]{2,0,1:T(8,128)(2,1)S(1)} %get-tuple-element.339) | copy-start | bytes 344068 | tf_op jit(solution)/shard_map/while
  375.9 2.8 copy-start.2
  393.1 2.5 copy-start.1
  393.1 2.5 copy-start.3
  393.1 2.5 copy-start.4
  395.6 1.1 copy-start.7
  396.0 0.7 copy-start.5
  396.7 9.6 %copy-start.6 = (bf16[224,2,128]{2,0,1:T(8,128)(2,1)}, bf16[224,2,128]{2,0,1:T(8,128)(2,1)S(1)}, u32[]{:S(2)}) copy-start(bf16[224,2,128]{2,0,1:T(8,128)(2,1)S(1)} %get-tuple-element.339) | copy-start | bytes 344068 | tf_op jit(solution)/shard_map/while
  403.5 2.8 copy-start.2
  420.7 2.5 copy-start.1
  420.7 2.5 copy-start.3
  420.7 2.5 copy-start.4
  423.2 1.2 copy-start.7
  424.4 9.6 %copy-start.6 = (bf16[224,2,128]{2,0,1:T(8,128)(2,1)}, bf16[224,2,128]{2,0,1:T(8,128)(2,1)S(1)}, u32[]{:S(2)}) copy-start(bf16[224,2,128]{2,0,1:T(8,128)(2,1)S(1)} %get-tuple-element.339) | copy-start | bytes 344068 | tf_op jit(solution)/shard_map/while
  431.2 2.8 copy-start.2
  448.3 2.5 copy-start.1
  448.4 2.5 copy-start.3
  448.4 2.5 copy-start.4
  450.9 1.1 copy-start.7
  451.2 0.7 copy-start.5
  452.0 9.6 %copy-start.6 = (bf16[224,2,128]{2,0,1:T(8,128)(2,1)}, bf16[224,2,128]{2,0,1:T(8,128)(2,1)S(1)}, u32[]{:S(2)}) copy-start(bf16[224,2,128]{2,0,1:T(8,128)(2,1)S(1)} %get-tuple-element.339) | copy-start | bytes 344068 | tf_op jit(solution)/shard_map/while
  458.8 2.8 copy-start.2
  476.0 2.5 copy-start.1
  476.0 2.5 copy-start.3
  476.0 2.5 copy-start.4
  478.5 1.2 copy-start.7
  479.7 9.6 %copy-start.6 = (bf16[224,2,128]{2,0,1:T(8,128)(2,1)}, bf16[224,2,128]{2,0,1:T(8,128)(2,1)S(1)}, u32[]{:S(2)}) copy-start(bf16[224,2,128]{2,0,1:T(8,128)(2,1)S(1)} %get-tuple-element.339) | copy-start | bytes 344068 | tf_op jit(solution)/shard_map/while
  486.5 2.8 copy-start.2
  503.7 2.5 copy-start.1
  503.7 2.5 copy-start.3
  503.7 2.5 copy-start.4
  506.2 1.1 copy-start.7
  507.3 9.6 %copy-start.6 = (bf16[224,2,128]{2,0,1:T(8,128)(2,1)}, bf16[224,2,128]{2,0,1:T(8,128)(2,1)S(1)}, u32[]{:S(2)}) copy-start(bf16[224,2,128]{2,0,1:T(8,128)(2,1)S(1)} %get-tuple-element.339) | copy-start | bytes 344068 | tf_op jit(solution)/shard_map/while
  514.1 2.8 copy-start.2
  531.3 2.5 copy-start.1
  531.3 2.5 copy-start.3
  531.3 2.5 copy-start.4
  533.8 1.2 copy-start.7
  535.0 9.6 %copy-start.6 = (bf16[224,2,128]{2,0,1:T(8,128)(2,1)}, bf16[224,2,128]{2,0,1:T(8,128)(2,1)S(1)}, u32[]{:S(2)}) copy-start(bf16[224,2,128]{2,0,1:T(8,128)(2,1)S(1)} %get-tuple-element.339) | copy-start | bytes 344068 | tf_op jit(solution)/shard_map/while
  541.8 2.8 copy-start.2
  559.0 2.5 copy-start.1
  559.0 2.5 copy-start.3
  559.0 2.5 copy-start.4
  561.5 1.1 copy-start.7
  562.6 9.6 %copy-start.6 = (bf16[224,2,128]{2,0,1:T(8,128)(2,1)}, bf16[224,2,128]{2,0,1:T(8,128)(2,1)S(1)}, u32[]{:S(2)}) copy-start(bf16[224,2,128]{2,0,1:T(8,128)(2,1)S(1)} %get-tuple-element.339) | copy-start | bytes 344068 | tf_op jit(solution)/shard_map/while
  569.4 2.8 copy-start.2
  586.6 2.5 copy-start.1
  586.6 2.5 copy-start.3
  586.6 2.5 copy-start.4
  589.1 1.2 copy-start.7
  590.3 31.8 %copy-start.11 = (f32[1536]{0:T(1024)S(1)}, f32[1536]{0:T(1024)}, u32[]{:S(2)}) copy-start(f32[1536]{0:T(1024)} %param.18) | copy-start | bytes 18436
  592.4 18.0 %all-to-all-start.6 = ((bf16[4,56,256]{2,1,0:T(8,128)(2,1)}), bf16[4,56,256]{2,1,0:T(8,128)(2,1)S(1)}, u32[]{:S(2)}, u32[]{:S(2)}) async-start(bf16[4,56,256]{2,1,0:T(8,128)(2,1)} %convert_element_type.30), calls=%async_computation.6 | async-start | bytes 229376 | tf_op jit(solution)/shard_map/all_to_all | solution.py:103
  610.4 11.7 %all-to-all-start.7 = ((bf16[4,56,256]{2,1,0:T(8,128)(2,1)}), bf16[4,56,256]{2,1,0:T(8,128)(2,1)S(1)}, u32[]{:S(2)}, u32[]{:S(2)}) async-start(bf16[4,56,256]{2,1,0:T(8,128)(2,1)} %convert_element_type.33), calls=%async_computation.7 | async-start | bytes 229376 | tf_op jit(solution)/shard_map/all_to_all | solution.py:104
  622.1 1.3 copy-start.12
  (6 other events, 4.3 us)
Sparse Core Ops, SparseCore 0:
  25.9 83.3 all-gather.8
  112.4 83.4 all-gather.10
  199.1 83.4 all-gather.4
  285.6 83.4 all-gather.6
where the time goes:
time: 635 us; the launch traced here: 631 us
  waiting for transfers between devices  308 us (49%)
  local copies, waits for them, and re-layouts  114 us (18%)
  matrix products  95.8 us (15%)
  blocking collectives  51.6 us (8%)
  starting transfers between devices  23.7 us (4%)
  other arithmetic  23.4 us (4%)
  between operations  13.9 us (2%)
    dynamic_slice x48, local copies, waits for them, and re-layouts, local(): final_state, ignored = lax.scan(one_block, start_state, stacked)  99.2 us
    all_gather x1, waiting for transfers between devices, local(): lax.all_gather(key_rows, 'seq', axis=0, tiled=True)  86.7 us
    all_gather x1, waiting for transfers between devices, local(): lax.all_gather(value_tangent, 'seq', axis=0, tiled=True)  86.7 us
    all_gather x1, waiting for transfers between devices, local(): lax.all_gather(key_tangent, 'seq', axis=0, tiled=True)  86.5 us
    dot_general x8, matrix products, absorb(): jnp.einsum('qhd,khd->hqk', query_heads, key_dot, preferred_element_type=j...  24.7 us
    reduce_sum x8, other arithmetic, absorb(): row_total = row_total * rescale + jnp.sum(weight_wide, axis=-1)  22 us
    all_gather x1, waiting for transfers between devices, local(): lax.all_gather(values, 'seq', axis=0, tiled=True)  21.7 us
    dot_general x8, matrix products, absorb(): jnp.einsum('qhd,khd->hqk', query_heads, key_head, preferred_element_type=...  20.3 us
  transfers between devices with their start and end apart: 8, of which 8 were waited for; matrix products, arithmetic and copies ran while one was open for 1% of the time, Pallas kernels for 0%

commit v1 on v0

v1 whole, which is shorter than its diff:
```python
import functools

import jax
import jax.numpy as jnp
from jax import lax
from jax.experimental import pallas as pl
from jax.experimental.pallas import tpu as pltpu
from jax.sharding import PartitionSpec as P

HD = 128
VMEM_LIMIT = 64 * 1024 * 1024
MESH = pl.DeviceIdType.MESH
SCALE = HD**-0.5
LOG2E = 1.4426950408889634
F32 = jnp.float32
BF16 = jnp.bfloat16
NEAR, FAR = 0, 1
LEFTWARD, RIGHTWARD = 0, 1


def kernel(
    nx,
    nz,
    q_hbm,
    k_hbm,
    v_hbm,
    qd_hbm,
    kd_hbm,
    vd_hbm,
    w_hbm,
    gate_hbm,
    gate_dot_hbm,
    out_ref,
    out_dot_ref,
    staged,
    gates,
    send_kv,
    send_q,
    land_kv,
    land_q,
    kv,
    q_all,
    acc,
    acc_shaded,
    row_max,
    row_total,
    tilt_sum,
    out_send,
    out_land,
    weight,
    staged_sems,
    gate_sems,
    weight_sem,
    kv_sems,
    q_sems,
    out_sems,
    ring_send_sems,
    ring_recv_sems,
    pair_send_sems,
    pair_recv_sems,
):
    tokens = q_hbm.shape[0]
    group = 2 * nx
    far_rows = nx * tokens
    half = nz // 2
    dp = lax.axis_index("dp")
    seq = lax.axis_index("seq")
    head_axis = lax.axis_index("head")
    z, x = seq // nx, seq % nx
    y, core = head_axis // 2, head_axis % 2

    def device(z_at, y_at, x_at, core_at):
        return (dp, z_at * nx + x_at, y_at * 2 + core_at)

    def taker(j):
        return device(z, (y + j // nx) % 2, (x + j % nx) % nx, core)

    def giver(j):
        return device(z, (y + j // nx) % 2, (x + nx - j % nx) % nx, core)

    def head_of(j):
        return ((y + j // nx) % 2) * nx + (x + j % nx) % nx

    right = device((z + 1) % nz, y, x, core)
    left = device((z + nz - 1) % nz, y, x, core)
    sibling = device(z, y, x, 1 - core)

    staged_copies = [
        pltpu.make_async_copy(ref, staged.at[i], staged_sems.at[i])
        for i, ref in enumerate((k_hbm, kd_hbm, v_hbm, vd_hbm, q_hbm, qd_hbm))
    ]
    for copy in staged_copies:
        copy.start()
    weight_copies = [
        pltpu.make_async_copy(gate_hbm, gates.at[0, 0], gate_sems.at[0]),
        pltpu.make_async_copy(gate_dot_hbm, gates.at[1, 0], gate_sems.at[1]),
    ]
    for copy in weight_copies:
        copy.start()
    for j in range(group):
        rows = pl.ds(pl.multiple_of(head_of(j) * HD, HD), HD)
        copy = pltpu.make_async_copy(
            w_hbm.at[rows], weight.at[pl.ds(j * HD, HD)], weight_sem.at[j]
        )
        copy.start()
        weight_copies.append(copy)

    barrier = pltpu.get_barrier_semaphore()
    partners = [taker(j) for j in range(1, group)] + [sibling, right]
    if nz > 2:
        partners.append(left)
    for partner in partners:
        pl.semaphore_signal(barrier, inc=1, device_id=partner, device_id_type=MESH)

    for copy in staged_copies:
        copy.wait()
    for j in range(group):
        columns = pl.ds(pl.multiple_of(head_of(j) * HD, HD), HD)
        send_kv[j] = jnp.concatenate(
            [staged[i, :, columns].astype(F32) for i in range(4)], axis=0
        ).astype(BF16)
        send_q[j] = jnp.concatenate(
            [staged[i, :, columns].astype(F32) for i in (4, 5)], axis=0
        ).astype(BF16)

    pl.semaphore_wait(barrier, len(partners))

    def remote(src, dst, send_sem, recv_sem, to):
        return pltpu.make_async_remote_copy(
            src_ref=src,
            dst_ref=dst,
            send_sem=send_sem,
            recv_sem=recv_sem,
            device_id=to,
            device_id_type=MESH,
        )

    kv_copies = [
        None
        if j == 0
        else remote(send_kv.at[j], land_kv.at[j], kv_sems.at[0, j], kv_sems.at[1, j], taker(j))
        for j in range(group)
    ]
    q_copies = [
        None
        if j == 0
        else remote(send_q.at[j], land_q.at[j], q_sems.at[0, j], q_sems.at[1, j], taker(j))
        for j in range(group)
    ]
    for j in range(1, nx):
        kv_copies[j].start()
    for j in range(nx, group):
        q_copies[j].start()
        kv_copies[j].start()
    for j in range(1, nx):
        q_copies[j].start()

    def slot(way, step):
        if step == 0:
            return half - 1, 0
        if step == half:
            return half - 1, 1
        return step - 1, way

    def steps_of(piece, way):
        return half if (piece == NEAR) == (way == RIGHTWARD) else half - 1

    ring_copies = {}
    pair_copies = {}
    for piece in (NEAR, FAR):
        for way in (LEFTWARD, RIGHTWARD):
            for step in range(1, steps_of(piece, way) + 1):
                for part in (0, 1):
                    from_p, from_sub = slot(way, step - 1)
                    to_p, to_sub = slot(way, step)
                    ring_copies[piece, way, step, part] = remote(
                        kv.at[piece, from_p, part, from_sub],
                        kv.at[piece, to_p, part, to_sub],
                        ring_send_sems.at[piece, way, step - 1, part],
                        ring_recv_sems.at[piece, way, step - 1, part],
                        right if way == RIGHTWARD else left,
                    )
        for p in range(half):
            for sub in (0, 1):
                for part in (0, 1):
                    pair_copies[piece, p, sub, part] = remote(
                        kv.at[piece, p, part, sub],
                        kv.at[piece, p, part, 2 + sub],
                        pair_send_sems.at[piece, p, sub, part],
                        pair_recv_sems.at[piece, p, sub, part],
                        sibling,
                    )

    def start_piece(piece):
        members = range(piece * nx, (piece + 1) * nx)
        for j in members:
            if j > 0:
                kv_copies[j].wait_recv()
        blocks = [(send_kv if j == 0 else land_kv)[j].astype(F32) for j in members]
        for part in (0, 1):
            for side in (0, 1):
                at = (2 * part + side) * tokens
                kv[piece, half - 1, part, 0, :, side * HD : (side + 1) * HD] = jnp.concatenate(
                    [block[at : at + tokens] for block in blocks], axis=0
                ).astype(BF16)
        for part in (0, 1):
            for way in (RIGHTWARD, LEFTWARD):
                if steps_of(piece, way) >= 1:
                    ring_copies[piece, way, 1, part].start()
        for part in (0, 1):
            pair_copies[piece, half - 1, 0, part].start()

    def pass_on(piece, step):
        for part in (0, 1):
            for way in (RIGHTWARD, LEFTWARD):
                if step <= steps_of(piece, way):
                    ring_copies[piece, way, step, part].wait_recv()
                    if step + 1 <= steps_of(piece, way):
                        ring_copies[piece, way, step + 1, part].start()
                    p, sub = slot(way, step)
                    pair_copies[piece, p, sub, part].start()

    def gather_queries():
        if gathered:
            return
        gathered.append(True)
        for j in range(1, group):
            q_copies[j].wait_recv()
        for side, at in ((0, tokens), (1, 0)):
            q_all[:, side * HD : (side + 1) * HD] = jnp.concatenate(
                [
                    (send_q if j == 0 else land_q)[j].astype(F32)[at : at + tokens]
                    for j in range(group)
                ],
                axis=0,
            ).astype(BF16)

    def absorb(piece, p, chunk):
        rows = pl.ds(pl.multiple_of(chunk * far_rows, 8), far_rows)
        query_rows = pl.ds(pl.multiple_of(chunk * far_rows, 16), far_rows)
        keys = kv[piece, p, 0].reshape(4 * far_rows, 2 * HD)
        vals = kv[piece, p, 1].reshape(4 * far_rows, 2 * HD)
        both = q_all[query_rows, :]
        transposed = (((1,), (1,)), ((), ()))
        scores = lax.dot_general(
            both[:, HD:], keys[:, :HD], transposed, preferred_element_type=F32
        ) * (SCALE * LOG2E)
        score_tangent = lax.dot_general(both, keys, transposed, preferred_element_type=F32)
        max_was = row_max[rows, :][:, :1]
        max_now = jnp.maximum(max_was, jnp.max(scores, axis=-1, keepdims=True))
        rescale = jnp.exp2(max_was - max_now)
        weights = jnp.exp2(scores - max_now).astype(BF16)
        wide = weights.astype(F32)
        shifted = wide * score_tangent
        shaded = shifted.astype(BF16)
        row_max[rows, :] = jnp.broadcast_to(max_now, (far_rows, HD))
        row_total[rows, :] = row_total[rows, :] * rescale + jnp.sum(wide, axis=-1, keepdims=True)
        tilt_sum[rows, :] = tilt_sum[rows, :] * rescale + jnp.sum(shifted, axis=-1, keepdims=True)
        acc[rows, :] = acc[rows, :] * rescale + jnp.dot(weights, vals, preferred_element_type=F32)
        acc_shaded[rows, :] = acc_shaded[rows, :] * rescale + jnp.dot(
            shaded, vals[:, :HD], preferred_element_type=F32
        )

    def absorb_all(piece, p):
        for sub in (0, 1):
            for part in (0, 1):
                pair_copies[piece, p, sub, part].wait_recv()

        def one(chunk, carry):
            absorb(piece, p, chunk)
            return carry

        lax.fori_loop(0, 2, one, 0)

    row_max[...] = jnp.full(row_max.shape, -1e30, F32)
    row_total[...] = jnp.zeros(row_total.shape, F32)
    tilt_sum[...] = jnp.zeros(tilt_sum.shape, F32)
    acc[...] = jnp.zeros(acc.shape, F32)
    acc_shaded[...] = jnp.zeros(acc_shaded.shape, F32)

    start_piece(NEAR)
    order = [(NEAR, step) for step in range(1, min(half, 2) + 1)] + [(FAR, 0)]
    near_left = [(NEAR, step) for step in range(3, half + 1)]
    far_left = [(FAR, step) for step in range(1, half + 1)]
    while near_left or far_left:
        if near_left:
            order.append(near_left.pop(0))
        if far_left:
            order.append(far_left.pop(0))
    ready = []
    gathered = []
    for at, (piece, step) in enumerate(order):
        last = at == len(order) - 1
        if last:
            gather_queries()
            while ready:
                absorb_all(*ready.pop(0))
        if step == 0:
            start_piece(piece)
            continue
        pass_on(piece, step)
        if ready and not last:
            gather_queries()
            absorb_all(*ready.pop(0))
        ready.append((piece, step - 1))

    (piece, p), = ready
    for sub in (0, 1):
        for part in (0, 1):
            pair_copies[piece, p, sub, part].wait_recv()
    out_copies = [
        None
        if j == 0
        else remote(out_send.at[j], out_land.at[j], out_sems.at[0, j], out_sems.at[1, j], giver(j))
        for j in range(group)
    ]
    for chunk in (1, 0):
        absorb(piece, p, chunk)
        rows = slice(chunk * far_rows, (chunk + 1) * far_rows)
        inverse = 1.0 / row_total[rows, :]
        attended = acc[rows, :HD] * inverse
        tangent = acc[rows, HD:] + SCALE * acc_shaded[rows, :]
        attended_dot = tangent * inverse - (SCALE * tilt_sum[rows, :] * inverse) * attended
        for at in range(nx):
            j = chunk * nx + at
            own = slice(at * tokens, (at + 1) * tokens)
            block = jnp.concatenate([attended[own], attended_dot[own]], axis=0).astype(BF16)
            if j == 0:
                out_land[j] = block
            else:
                out_send[j] = block
                out_copies[j].start()

    for copy in weight_copies:
        copy.wait()
    for j in range(1, group):
        out_copies[j].wait_recv()
    everything = jnp.concatenate([out_land[j] for j in range(group)], axis=1)
    projected = jnp.dot(everything, weight[...], preferred_element_type=F32)
    primal, dot = projected[:tokens], projected[tokens:]
    gate, gate_dot = gates[0], gates[1]
    out_ref[...] = (gate * primal).astype(BF16)
    out_dot_ref[...] = (gate_dot * primal + gate * dot).astype(BF16)

    for j in range(1, group):
        kv_copies[j].wait_send()
        q_copies[j].wait_send()
        out_copies[j].wait_send()
    for copy in ring_copies.values():
        copy.wait_send()
    for copy in pair_copies.values():
        copy.wait_send()


def local(
    queries,
    key_rows,
    values,
    query_tangent,
    key_tangent,
    value_tangent,
    out_weight,
    gate_vector,
    gate_tangent,
    *,
    seq_size,
):
    tokens = queries.shape[0]
    group = queries.shape[1] // HD
    nx = group // 2
    nz = seq_size // nx
    width = out_weight.shape[1]
    rows = group * tokens
    piece_rows = nx * tokens
    half = nz // 2
    vmem = pl.BlockSpec(memory_space=pltpu.VMEM)
    out_shape = jax.ShapeDtypeStruct((tokens, width), BF16)
    all_rows = rows * nz * 2
    return pl.pallas_call(
        functools.partial(kernel, nx, nz),
        out_shape=(out_shape, out_shape),
        in_specs=[pl.BlockSpec(memory_space=pl.ANY)] * 9,
        out_specs=(vmem, vmem),
        scratch_shapes=[
            pltpu.VMEM((6, tokens, group * HD), BF16),
            pltpu.VMEM((2, 1, width), F32),
            pltpu.VMEM((group, 4 * tokens, HD), BF16),
            pltpu.VMEM((group, 2 * tokens, HD), BF16),
            pltpu.VMEM((group, 4 * tokens, HD), BF16),
            pltpu.VMEM((group, 2 * tokens, HD), BF16),
            pltpu.VMEM((2, half, 2, 4, piece_rows, 2 * HD), BF16),
            pltpu.VMEM((rows, 2 * HD), BF16),
            pltpu.VMEM((rows, 2 * HD), F32),
            pltpu.VMEM((rows, HD), F32),
            pltpu.VMEM((rows, HD), F32),
            pltpu.VMEM((rows, HD), F32),
            pltpu.VMEM((rows, HD), F32),
            pltpu.VMEM((group, 2 * tokens, HD), BF16),
            pltpu.VMEM((group, 2 * tokens, HD), BF16),
            pltpu.VMEM((group * HD, width), BF16),
            pltpu.SemaphoreType.DMA((6,)),
            pltpu.SemaphoreType.DMA((2,)),
            pltpu.SemaphoreType.DMA((group,)),
            pltpu.SemaphoreType.DMA((2, group)),
            pltpu.SemaphoreType.DMA((2, group)),
            pltpu.SemaphoreType.DMA((2, group)),
            pltpu.SemaphoreType.DMA((2, 2, half, 2)),
            pltpu.SemaphoreType.DMA((2, 2, half, 2)),
            pltpu.SemaphoreType.DMA((2, half, 2, 2)),
            pltpu.SemaphoreType.DMA((2, half, 2, 2)),
        ],
        compiler_params=pltpu.CompilerParams(
            collective_id=0, has_side_effects=True, vmem_limit_bytes=VMEM_LIMIT
        ),
        cost_estimate=pl.CostEstimate(
            flops=12 * rows * all_rows * HD,
            bytes_accessed=16 * all_rows * HD,
            transcendentals=rows * all_rows,
        ),
    )(
        queries,
        key_rows,
        values,
        query_tangent,
        key_tangent,
        value_tangent,
        out_weight,
        gate_vector,
        gate_tangent,
    )


def solution(mesh):
    rows = P(("dp", "seq", "head"), None)
    return jax.shard_map(
        functools.partial(local, seq_size=mesh.shape["seq"]),
        mesh=mesh,
        in_specs=(rows,) * 6 + (P(), P("dp"), P("dp")),
        out_specs=(rows, rows),
        check_vma=False,
    )
```

time: 635 us -> 80.5 us (0.13)
  waiting for transfers between devices: 308 us -> 0 us
  local copies, waits for them, and re-layouts: 114 us -> 3.2 us
  matrix products: 95.8 us -> 0 us
  Pallas kernels: 0 us -> 76.5 us
  blocking collectives: 51.6 us -> 0 us
  starting transfers between devices: 23.7 us -> 0 us
  other arithmetic: 23.4 us -> 0 us
  between operations: 13.9 us -> 0.64 us
    all_gather x4 -> x0, waiting for transfers between devices: 282 us -> none  [the longest x1 86.7 us: local(): lax.all_gather(key_rows, 'seq', axis=0, tiled=True)]
    dynamic_slice x48 -> x0, local copies, waits for them, and re-layouts: 99.2 us -> none  [local(): final_state, ignored = lax.scan(one_block, start_state, stacked)]
    dot_general x50 -> x0, matrix products: 95.8 us -> none  [the longest x8 24.7 us: absorb(): jnp.einsum('qhd,khd->hqk', query_heads, key_dot, preferred_element_type=j...]
    pallas_call x0 -> x1, Pallas kernels: none -> 76.5 us  [local(): pl.pallas_call(functools.partial(kernel, nx, nz), out_shape=(out_shape, o...]
    all_to_all x4 -> x0, blocking collectives: 51.6 us -> none  [the longest x1 17.4 us: local(): lax.all_to_all(values, 'head', split_axis=1, concat_axis=0, tiled=True)]
    all_to_all x4 -> x0, waiting for transfers between devices: 26.4 us -> none  [the longest x1 7.36 us: local(): lax.all_to_all(attended_tangent, 'head', split_axis=0, concat_axis=1, til...]
    all_to_all x4 -> x0, starting transfers between devices: 23.5 us -> none  [the longest x1 10.7 us: local(): lax.all_to_all(attended, 'head', split_axis=0, concat_axis=1, tiled=True)]
    reduce_sum x8 -> x0, other arithmetic: 22 us -> none  [absorb(): row_total = row_total * rescale + jnp.sum(weight_wide, axis=-1)]
  transfers between devices with their start and end apart: 8 -> 0, of which waited for: 8 -> 0; matrix products, arithmetic and copies ran while one was open for 1% -> 0% of each run, Pallas kernels for 0% -> 0%
where the time goes in v1:
time: 80.5 us; the launch traced here: 80.3 us
  Pallas kernels  76.5 us (95%)
  local copies, waits for them, and re-layouts  3.2 us (4%)
    pallas_call x1, Pallas kernels, local(): pl.pallas_call(functools.partial(kernel, nx, nz), out_shape=(out_shape, o...  76.5 us
    unnamed x2, local copies, waits for them, and re-layouts  3.2 us

profile of v1, /device:TPU:1, one launch (start us, length us, event | category | flops | bytes accessed | tf_op | source)
XLA Modules:
  0.0 80.3 jit_solution(15221927486955741279)
XLA Ops:
  0.6 76.5 %shard_map.104 = (bf16[56,1536]{1,0:T(8,128)(2,1)}, bf16[56,1536]{1,0:T(8,128)(2,1)}) custom-call(bf16[56,1024]{1,0:T(8,128)(2,1)} %q_hbm.1, bf16[56,1024]{1,0:T(8,128)(2,1)} %k_hbm.1, bf16[56,1024]{1,0:T(8,128)(2,1)} %v_hbm.1, bf16[56,1024]{1,0:T(8,128)(2,1)} %qd_hbm.1, bf16[56,1024]{1,0:T(8,128)(2,1)} %kd_hbm.1, bf16[56,1024]{1,0:T(8,128)(2,1)} %vd_hbm.1, ...), custom_call_target="tpu_custom_call" | custom-call | flops 4932501504 | bytes 14680064 | tf_op jit(solution)/shard_map/pallas_call | solution.py:379
  77.1 1.6 %copy.13 = bf16[56,1536]{1,0:T(8,128)(2,1)} copy(bf16[56,1536]{1,0:T(8,128)(2,1)} %get-tuple-element.4) | data formatting | bytes 344064
  78.7 1.6 %copy.14 = bf16[56,1536]{1,0:T(8,128)(2,1)} copy(bf16[56,1536]{1,0:T(8,128)(2,1)} %get-tuple-element.5) | data formatting | bytes 344064

commit v2 on v1

--- a/solution.py
+++ b/solution.py
@@ -38,6 +38,8 @@
     send_q,
     land_kv,
     land_q,
+    relay_kv,
+    relay_q,
     kv,
     q_all,
     acc,
@@ -53,6 +55,8 @@
     weight_sem,
     kv_sems,
     q_sems,
+    relay_kv_sems,
+    relay_q_sems,
     out_sems,
     ring_send_sems,
     ring_recv_sems,
@@ -71,6 +75,12 @@
 
     def device(z_at, y_at, x_at, core_at):
         return (dp, z_at * nx + x_at, y_at * 2 + core_at)
+
+    other_dp = (dp + 2) % 4
+    other_y = ((y + (dp + 2) // 4) % 2, (y + (dp + 2) // 4 + 1) % 2)
+
+    def along_y(way, dx):
+        return (other_dp, z * nx + (x + dx) % nx, other_y[way] * 2 + core)
 
     def taker(j):
         return device(z, (y + j // nx) % 2, (x + j % nx) % nx, core)
@@ -107,6 +117,7 @@
 
     barrier = pltpu.get_barrier_semaphore()
     partners = [taker(j) for j in range(1, group)] + [sibling, right]
+    partners += [along_y(way, dx) for way in (0, 1) for dx in range(nx)]
     if nz > 2:
         partners.append(left)
     for partner in partners:
@@ -116,9 +127,10 @@
         copy.wait()
     for j in range(group):
         columns = pl.ds(pl.multiple_of(head_of(j) * HD, HD), HD)
-        send_kv[j] = jnp.concatenate(
-            [staged[i, :, columns].astype(F32) for i in range(4)], axis=0
-        ).astype(BF16)
+        for part in (0, 1):
+            send_kv[part, j] = jnp.concatenate(
+                [staged[i, :, columns].astype(F32) for i in (2 * part, 2 * part + 1)], axis=0
+            ).astype(BF16)
         send_q[j] = jnp.concatenate(
             [staged[i, :, columns].astype(F32) for i in (4, 5)], axis=0
         ).astype(BF16)
@@ -135,25 +147,72 @@
             device_id_type=MESH,
         )
 
-    kv_copies = [
-        None
-        if j == 0
-        else remote(send_kv.at[j], land_kv.at[j], kv_sems.at[0, j], kv_sems.at[1, j], taker(j))
-        for j in range(group)
+    near_kv = [
+        remote(
+            send_kv.at[:, j], land_kv.at[:, j], kv_sems.at[0, 0, j], kv_sems.at[1, 0, j], taker(j)
+        )
+        for j in range(1, nx)
     ]
-    q_copies = [
-        None
-        if j == 0
-        else remote(send_q.at[j], land_q.at[j], q_sems.at[0, j], q_sems.at[1, j], taker(j))
-        for j in range(group)
+    near_q = [
+        remote(send_q.at[j], land_q.at[j], q_sems.at[0, j], q_sems.at[1, j], taker(j))
+        for j in range(1, nx)
     ]
-    for j in range(1, nx):
-        kv_copies[j].start()
-    for j in range(nx, group):
-        q_copies[j].start()
-        kv_copies[j].start()
-    for j in range(1, nx):
-        q_copies[j].start()
+    q_split = ((0, (nx + 1) // 2), ((nx + 1) // 2, nx))
+    leg_q, leg_kv, far_q, far_kv = [], [], [], []
+    for way in (0, 1):
+        low, high = q_split[way]
+        leg_kv.append(
+            remote(
+                send_kv.at[way, pl.ds(nx, nx)],
+                relay_kv.at[way],
+                relay_kv_sems.at[0, way],
+                relay_kv_sems.at[1, way],
+                along_y(way, 0),
+            )
+        )
+        far_kv.append(
+            [
+                remote(
+                    relay_kv.at[way, dx],
+                    land_kv.at[way, nx + dx],
+                    kv_sems.at[0, way, nx + dx],
+                    kv_sems.at[1, way, nx + dx],
+                    along_y(way, dx),
+                )
+                for dx in range(nx)
+            ]
+        )
+        if high > low:
+            leg_q.append(
+                remote(
+                    send_q.at[pl.ds(nx + low, high - low)],
+                    relay_q.at[pl.ds(low, high - low)],
+                    relay_q_sems.at[0, way],
+                    relay_q_sems.at[1, way],
+                    along_y(way, 0),
+                )
+            )
+            far_q.append(
+                [
+                    remote(
+                        relay_q.at[dx],
+                        land_q.at[nx + dx],
+                        q_sems.at[0, nx + dx],
+                        q_sems.at[1, nx + dx],
+                        along_y(way, dx),
+                    )
+                    for dx in range(low, high)
+                ]
+            )
+    for copy in near_kv + leg_q + leg_kv + near_q:
+        copy.start()
+
+    def relay():
+        for legs, onward in ((leg_q, far_q), (leg_kv, far_kv)):
+            for leg, copies in zip(legs, onward):
+                leg.wait_recv()
+                for copy in copies:
+                    copy.start()
 
     def slot(way, step):
         if step == 0:
@@ -193,13 +252,12 @@
 
     def start_piece(piece):
         members = range(piece * nx, (piece + 1) * nx)
-        for j in members:
-            if j > 0:
-                kv_copies[j].wait_recv()
-        blocks = [(send_kv if j == 0 else land_kv)[j].astype(F32) for j in members]
+        for copy in near_kv if piece == NEAR else far_kv[0] + far_kv[1]:
+            copy.wait_recv()
         for part in (0, 1):
+            blocks = [(send_kv if j == 0 else land_kv)[part, j].astype(F32) for j in members]
             for side in (0, 1):
-                at = (2 * part + side) * tokens
+                at = side * tokens
                 kv[piece, half - 1, part, 0, :, side * HD : (side + 1) * HD] = jnp.concatenate(
                     [block[at : at + tokens] for block in blocks], axis=0
                 ).astype(BF16)
@@ -224,8 +282,9 @@
         if gathered:
             return
         gathered.append(True)
-        for j in range(1, group):
-            q_copies[j].wait_recv()
+        for copies in [near_q] + far_q:
+            for copy in copies:
+                copy.wait_recv()
         for side, at in ((0, tokens), (1, 0)):
             q_all[:, side * HD : (side + 1) * HD] = jnp.concatenate(
                 [
@@ -279,6 +338,7 @@
     acc_shaded[...] = jnp.zeros(acc_shaded.shape, F32)
 
     start_piece(NEAR)
+    relay()
     order = [(NEAR, step) for step in range(1, min(half, 2) + 1)] + [(FAR, 0)]
     near_left = [(NEAR, step) for step in range(3, half + 1)]
     far_left = [(FAR, step) for step in range(1, half + 1)]
@@ -343,9 +403,10 @@
     out_dot_ref[...] = (gate_dot * primal + gate * dot).astype(BF16)
 
     for j in range(1, group):
-        kv_copies[j].wait_send()
-        q_copies[j].wait_send()
         out_copies[j].wait_send()
+    for copies in [near_kv, near_q, leg_kv, leg_q] + far_kv + far_q:
+        for copy in copies:
+            copy.wait_send()
     for copy in ring_copies.values():
         copy.wait_send()
     for copy in pair_copies.values():
@@ -384,10 +445,12 @@
         scratch_shapes=[
             pltpu.VMEM((6, tokens, group * HD), BF16),
             pltpu.VMEM((2, 1, width), F32),
-            pltpu.VMEM((group, 4 * tokens, HD), BF16),
+            pltpu.VMEM((2, group, 2 * tokens, HD), BF16),
             pltpu.VMEM((group, 2 * tokens, HD), BF16),
-            pltpu.VMEM((group, 4 * tokens, HD), BF16),
+            pltpu.VMEM((2, group, 2 * tokens, HD), BF16),
             pltpu.VMEM((group, 2 * tokens, HD), BF16),
+            pltpu.VMEM((2, nx, 2 * tokens, HD), BF16),
+            pltpu.VMEM((nx, 2 * tokens, HD), BF16),
             pltpu.VMEM((2, half, 2, 4, piece_rows, 2 * HD), BF16),
             pltpu.VMEM((rows, 2 * HD), BF16),
             pltpu.VMEM((rows, 2 * HD), F32),
@@ -401,8 +464,10 @@
             pltpu.SemaphoreType.DMA((6,)),
             pltpu.SemaphoreType.DMA((2,)),
             pltpu.SemaphoreType.DMA((group,)),
+            pltpu.SemaphoreType.DMA((2, 2, group)),
             pltpu.SemaphoreType.DMA((2, group)),
-            pltpu.SemaphoreType.DMA((2, group)),
+            pltpu.SemaphoreType.DMA((2, 2)),
+            pltpu.SemaphoreType.DMA((2, 2)),
             pltpu.SemaphoreType.DMA((2, group)),
             pltpu.SemaphoreType.DMA((2, 2, half, 2)),
             pltpu.SemaphoreType.DMA((2, 2, half, 2)),

time: 80.5 us -> 80.3 us (level)
  Pallas kernels: 76.5 us -> 75.6 us
    pallas_call x1, Pallas kernels: 76.5 us -> 75.6 us  [local(): pl.pallas_call(functools.partial(kernel, nx, nz), out_shape=(out_shape, o...]
where the time goes in v2:
time: 80.3 us; the launch traced here: 79.4 us
  Pallas kernels  75.6 us (94%)
  local copies, waits for them, and re-layouts  3.2 us (4%)
    pallas_call x1, Pallas kernels, local(): pl.pallas_call(functools.partial(kernel, nx, nz), out_shape=(out_shape, o...  75.6 us
    unnamed x2, local copies, waits for them, and re-layouts  3.2 us

profile of v2, /device:TPU:1, one launch (start us, length us, event | category | flops | bytes accessed | tf_op | source)
XLA Modules:
  0.0 79.4 jit_solution(17688964173144340316)
XLA Ops:
  0.6 75.6 %shard_map.104 = (bf16[56,1536]{1,0:T(8,128)(2,1)}, bf16[56,1536]{1,0:T(8,128)(2,1)}) custom-call(bf16[56,1024]{1,0:T(8,128)(2,1)} %q_hbm.1, bf16[56,1024]{1,0:T(8,128)(2,1)} %k_hbm.1, bf16[56,1024]{1,0:T(8,128)(2,1)} %v_hbm.1, bf16[56,1024]{1,0:T(8,128)(2,1)} %qd_hbm.1, bf16[56,1024]{1,0:T(8,128)(2,1)} %kd_hbm.1, bf16[56,1024]{1,0:T(8,128)(2,1)} %vd_hbm.1, ...), custom_call_target="tpu_custom_call" | custom-call | flops 4932501504 | bytes 14680064 | tf_op jit(solution)/shard_map/pallas_call | solution.py:440
  76.2 1.6 %copy.13 = bf16[56,1536]{1,0:T(8,128)(2,1)} copy(bf16[56,1536]{1,0:T(8,128)(2,1)} %get-tuple-element.4) | data formatting | bytes 344064
  77.8 1.6 %copy.14 = bf16[56,1536]{1,0:T(8,128)(2,1)} copy(bf16[56,1536]{1,0:T(8,128)(2,1)} %get-tuple-element.5) | data formatting | bytes 344064

commit v3 on v2

--- a/solution.py
+++ b/solution.py
@@ -225,7 +225,6 @@
         return half if (piece == NEAR) == (way == RIGHTWARD) else half - 1
 
     ring_copies = {}
-    pair_copies = {}
     for piece in (NEAR, FAR):
         for way in (LEFTWARD, RIGHTWARD):
             for step in range(1, steps_of(piece, way) + 1):
@@ -239,16 +238,15 @@
                         ring_recv_sems.at[piece, way, step - 1, part],
                         right if way == RIGHTWARD else left,
                     )
-        for p in range(half):
-            for sub in (0, 1):
-                for part in (0, 1):
-                    pair_copies[piece, p, sub, part] = remote(
-                        kv.at[piece, p, part, sub],
-                        kv.at[piece, p, part, 2 + sub],
-                        pair_send_sems.at[piece, p, sub, part],
-                        pair_recv_sems.at[piece, p, sub, part],
-                        sibling,
-                    )
+
+    def pair_copy(piece, p, sub, part):
+        return remote(
+            kv.at[piece, p, part, sub],
+            kv.at[piece, p, part, 2 + sub],
+            pair_send_sems.at[piece, p, sub, part],
+            pair_recv_sems.at[piece, p, sub, part],
+            sibling,
+        )
 
     def start_piece(piece):
         members = range(piece * nx, (piece + 1) * nx)
@@ -266,22 +264,19 @@
                 if steps_of(piece, way) >= 1:
                     ring_copies[piece, way, 1, part].start()
         for part in (0, 1):
-            pair_copies[piece, half - 1, 0, part].start()
+            pair_copy(piece, half - 1, 0, part).start()
 
     def pass_on(piece, step):
         for part in (0, 1):
-            for way in (RIGHTWARD, LEFTWARD):
+            for way in (RIGHTWARD, LEFTWARD) if piece == NEAR else (LEFTWARD, RIGHTWARD):
                 if step <= steps_of(piece, way):
                     ring_copies[piece, way, step, part].wait_recv()
                     if step + 1 <= steps_of(piece, way):
                         ring_copies[piece, way, step + 1, part].start()
                     p, sub = slot(way, step)
-                    pair_copies[piece, p, sub, part].start()
+                    pair_copy(piece, p, sub, part).start()
 
     def gather_queries():
-        if gathered:
-            return
-        gathered.append(True)
         for copies in [near_q] + far_q:
             for copy in copies:
                 copy.wait_recv()
@@ -294,42 +289,29 @@
                 axis=0,
             ).astype(BF16)
 
-    def absorb(piece, p, chunk):
-        rows = pl.ds(pl.multiple_of(chunk * far_rows, 8), far_rows)
-        query_rows = pl.ds(pl.multiple_of(chunk * far_rows, 16), far_rows)
+    def absorb(piece, p):
         keys = kv[piece, p, 0].reshape(4 * far_rows, 2 * HD)
         vals = kv[piece, p, 1].reshape(4 * far_rows, 2 * HD)
-        both = q_all[query_rows, :]
+        both = q_all[...]
         transposed = (((1,), (1,)), ((), ()))
         scores = lax.dot_general(
             both[:, HD:], keys[:, :HD], transposed, preferred_element_type=F32
         ) * (SCALE * LOG2E)
         score_tangent = lax.dot_general(both, keys, transposed, preferred_element_type=F32)
-        max_was = row_max[rows, :][:, :1]
+        max_was = row_max[...][:, :1]
         max_now = jnp.maximum(max_was, jnp.max(scores, axis=-1, keepdims=True))
         rescale = jnp.exp2(max_was - max_now)
         weights = jnp.exp2(scores - max_now).astype(BF16)
         wide = weights.astype(F32)
         shifted = wide * score_tangent
         shaded = shifted.astype(BF16)
-        row_max[rows, :] = jnp.broadcast_to(max_now, (far_rows, HD))
-        row_total[rows, :] = row_total[rows, :] * rescale + jnp.sum(wide, axis=-1, keepdims=True)
-        tilt_sum[rows, :] = tilt_sum[rows, :] * rescale + jnp.sum(shifted, axis=-1, keepdims=True)
-        acc[rows, :] = acc[rows, :] * rescale + jnp.dot(weights, vals, preferred_element_type=F32)
-        acc_shaded[rows, :] = acc_shaded[rows, :] * rescale + jnp.dot(
+        row_max[...] = jnp.broadcast_to(max_now, row_max.shape)
+        row_total[...] = row_total[...] * rescale + jnp.sum(wide, axis=-1, keepdims=True)
+        tilt_sum[...] = tilt_sum[...] * rescale + jnp.sum(shifted, axis=-1, keepdims=True)
+        acc[...] = acc[...] * rescale + jnp.dot(weights, vals, preferred_element_type=F32)
+        acc_shaded[...] = acc_shaded[...] * rescale + jnp.dot(
             shaded, vals[:, :HD], preferred_element_type=F32
         )
-
-    def absorb_all(piece, p):
-        for sub in (0, 1):
-            for part in (0, 1):
-                pair_copies[piece, p, sub, part].wait_recv()
-
-        def one(chunk, carry):
-            absorb(piece, p, chunk)
-            return carry
-
-        lax.fori_loop(0, 2, one, 0)
 
     row_max[...] = jnp.full(row_max.shape, -1e30, F32)
     row_total[...] = jnp.zeros(row_total.shape, F32)
@@ -339,35 +321,40 @@
 
     start_piece(NEAR)
     relay()
-    order = [(NEAR, step) for step in range(1, min(half, 2) + 1)] + [(FAR, 0)]
-    near_left = [(NEAR, step) for step in range(3, half + 1)]
-    far_left = [(FAR, step) for step in range(1, half + 1)]
-    while near_left or far_left:
-        if near_left:
-            order.append(near_left.pop(0))
-        if far_left:
-            order.append(far_left.pop(0))
-    ready = []
-    gathered = []
-    for at, (piece, step) in enumerate(order):
-        last = at == len(order) - 1
-        if last:
-            gather_queries()
-            while ready:
-                absorb_all(*ready.pop(0))
-        if step == 0:
-            start_piece(piece)
-            continue
-        pass_on(piece, step)
-        if ready and not last:
-            gather_queries()
-            absorb_all(*ready.pop(0))
-        ready.append((piece, step - 1))
-
-    (piece, p), = ready
-    for sub in (0, 1):
-        for part in (0, 1):
-            pair_copies[piece, p, sub, part].wait_recv()
+
+    before = {at: [] for at in range(2 * half)}
+    for step in range(1, min(half, 2) + 1):
+        before[0].append((NEAR, step))
+    at = 1
+    for step in range(1, half + 1):
+        if step + 2 <= half:
+            before[at].append((NEAR, step + 2))
+            at += 1
+        before[2 * half - 1 if step == half else at].append((FAR, step))
+        at += 1
+
+    def block(at, carry):
+        for now, arrivals in before.items():
+            if not arrivals:
+                continue
+
+            @pl.when(at == now)
+            def _(now=now, arrivals=arrivals):
+                for piece, step in arrivals:
+                    pass_on(piece, step)
+                if now == 0:
+                    start_piece(FAR)
+                    gather_queries()
+
+        piece, p = at // half, at % half
+        for sub in (0, 1):
+            for part in (0, 1):
+                pair_copy(piece, p, sub, part).wait_recv()
+        absorb(piece, p)
+        return carry
+
+    lax.fori_loop(0, 2 * half, block, 0)
+
     out_copies = [
         None
         if j == 0
@@ -375,7 +362,6 @@
         for j in range(group)
     ]
     for chunk in (1, 0):
-        absorb(piece, p, chunk)
         rows = slice(chunk * far_rows, (chunk + 1) * far_rows)
         inverse = 1.0 / row_total[rows, :]
         attended = acc[rows, :HD] * inverse
@@ -409,8 +395,11 @@
             copy.wait_send()
     for copy in ring_copies.values():
         copy.wait_send()
-    for copy in pair_copies.values():
-        copy.wait_send()
+    for piece in (NEAR, FAR):
+        for p in range(half):
+            for sub in (0, 1):
+                for part in (0, 1):
+                    pair_copy(piece, p, sub, part).wait_send()
 
 
 def local(

time: 80.3 us -> 80.8 us (level)
  the two profiles are of different devices: /device:TPU:1 before, /device:TPU:19 now
where the time goes in v3:
time: 80.8 us; the launch traced here: 80.6 us
  Pallas kernels  76.8 us (95%)
  local copies, waits for them, and re-layouts  3.2 us (4%)
    pallas_call x1, Pallas kernels, local(): pl.pallas_call(functools.partial(kernel, nx, nz), out_shape=(out_shape, o...  76.8 us
    unnamed x2, local copies, waits for them, and re-layouts  3.2 us

profile of v3, /device:TPU:19, one launch (start us, length us, event | category | flops | bytes accessed | tf_op | source)
XLA Modules:
  0.0 80.6 jit_solution(7979277186287211805)
XLA Ops:
  0.6 76.8 %shard_map.104 = (bf16[56,1536]{1,0:T(8,128)(2,1)}, bf16[56,1536]{1,0:T(8,128)(2,1)}) custom-call(bf16[56,1024]{1,0:T(8,128)(2,1)} %q_hbm.1, bf16[56,1024]{1,0:T(8,128)(2,1)} %k_hbm.1, bf16[56,1024]{1,0:T(8,128)(2,1)} %v_hbm.1, bf16[56,1024]{1,0:T(8,128)(2,1)} %qd_hbm.1, bf16[56,1024]{1,0:T(8,128)(2,1)} %kd_hbm.1, bf16[56,1024]{1,0:T(8,128)(2,1)} %vd_hbm.1, ...), custom_call_target="tpu_custom_call" | custom-call | flops 4932501504 | bytes 14680064 | tf_op jit(solution)/shard_map/pallas_call | solution.py:429
  77.4 1.6 %copy.13 = bf16[56,1536]{1,0:T(8,128)(2,1)} copy(bf16[56,1536]{1,0:T(8,128)(2,1)} %get-tuple-element.4) | data formatting | bytes 344064
  79.0 1.6 %copy.14 = bf16[56,1536]{1,0:T(8,128)(2,1)} copy(bf16[56,1536]{1,0:T(8,128)(2,1)} %get-tuple-element.5) | data formatting | bytes 344064

commit v4 on v3

--- a/solution.py
+++ b/solution.py
@@ -11,7 +11,6 @@
 VMEM_LIMIT = 64 * 1024 * 1024
 MESH = pl.DeviceIdType.MESH
 SCALE = HD**-0.5
-LOG2E = 1.4426950408889634
 F32 = jnp.float32
 BF16 = jnp.bfloat16
 NEAR, FAR = 0, 1
@@ -28,12 +27,8 @@
     kd_hbm,
     vd_hbm,
     w_hbm,
-    gate_hbm,
-    gate_dot_hbm,
     out_ref,
-    out_dot_ref,
     staged,
-    gates,
     send_kv,
     send_q,
     land_kv,
@@ -51,7 +46,6 @@
     out_land,
     weight,
     staged_sems,
-    gate_sems,
     weight_sem,
     kv_sems,
     q_sems,
@@ -101,12 +95,7 @@
     ]
     for copy in staged_copies:
         copy.start()
-    weight_copies = [
-        pltpu.make_async_copy(gate_hbm, gates.at[0, 0], gate_sems.at[0]),
-        pltpu.make_async_copy(gate_dot_hbm, gates.at[1, 0], gate_sems.at[1]),
-    ]
-    for copy in weight_copies:
-        copy.start()
+    weight_copies = []
     for j in range(group):
         rows = pl.ds(pl.multiple_of(head_of(j) * HD, HD), HD)
         copy = pltpu.make_async_copy(
@@ -225,26 +214,27 @@
         return half if (piece == NEAR) == (way == RIGHTWARD) else half - 1
 
     ring_copies = {}
+    part_rows = (pl.ds(0, far_rows // 2), pl.ds(far_rows // 2, far_rows // 2))
     for piece in (NEAR, FAR):
         for way in (LEFTWARD, RIGHTWARD):
             for step in range(1, steps_of(piece, way) + 1):
-                for part in (0, 1):
+                for part in range(4):
                     from_p, from_sub = slot(way, step - 1)
                     to_p, to_sub = slot(way, step)
                     ring_copies[piece, way, step, part] = remote(
-                        kv.at[piece, from_p, part, from_sub],
-                        kv.at[piece, to_p, part, to_sub],
+                        kv.at[piece, from_p, part // 2, from_sub, part_rows[part % 2]],
+                        kv.at[piece, to_p, part // 2, to_sub, part_rows[part % 2]],
                         ring_send_sems.at[piece, way, step - 1, part],
                         ring_recv_sems.at[piece, way, step - 1, part],
                         right if way == RIGHTWARD else left,
                     )
 
-    def pair_copy(piece, p, sub, part):
+    def pair_copy(piece, p, sub):
         return remote(
-            kv.at[piece, p, part, sub],
-            kv.at[piece, p, part, 2 + sub],
-            pair_send_sems.at[piece, p, sub, part],
-            pair_recv_sems.at[piece, p, sub, part],
+            kv.at[piece, p, :, sub],
+            kv.at[piece, p, :, 2 + sub],
+            pair_send_sems.at[piece, p, sub],
+            pair_recv_sems.at[piece, p, sub],
             sibling,
         )
 
@@ -259,22 +249,21 @@
                 kv[piece, half - 1, part, 0, :, side * HD : (side + 1) * HD] = jnp.concatenate(
                     [block[at : at + tokens] for block in blocks], axis=0
                 ).astype(BF16)
-        for part in (0, 1):
+        for part in range(4):
             for way in (RIGHTWARD, LEFTWARD):
                 if steps_of(piece, way) >= 1:
                     ring_copies[piece, way, 1, part].start()
-        for part in (0, 1):
-            pair_copy(piece, half - 1, 0, part).start()
+        pair_copy(piece, half - 1, 0).start()
 
     def pass_on(piece, step):
-        for part in (0, 1):
+        for part in range(4):
             for way in (RIGHTWARD, LEFTWARD) if piece == NEAR else (LEFTWARD, RIGHTWARD):
                 if step <= steps_of(piece, way):
                     ring_copies[piece, way, step, part].wait_recv()
                     if step + 1 <= steps_of(piece, way):
                         ring_copies[piece, way, step + 1, part].start()
-                    p, sub = slot(way, step)
-                    pair_copy(piece, p, sub, part).start()
+                    if part == 3:
+                        pair_copy(piece, *slot(way, step)).start()
 
     def gather_queries():
         for copies in [near_q] + far_q:
@@ -289,6 +278,12 @@
                 axis=0,
             ).astype(BF16)
 
+    def by_lane(block):
+        total = block[:, :HD]
+        for at in range(HD, block.shape[1], HD):
+            total = total + block[:, at : at + HD]
+        return total
+
     def absorb(piece, p):
         keys = kv[piece, p, 0].reshape(4 * far_rows, 2 * HD)
         vals = kv[piece, p, 1].reshape(4 * far_rows, 2 * HD)
@@ -296,18 +291,18 @@
         transposed = (((1,), (1,)), ((), ()))
         scores = lax.dot_general(
             both[:, HD:], keys[:, :HD], transposed, preferred_element_type=F32
-        ) * (SCALE * LOG2E)
+        ) * SCALE
         score_tangent = lax.dot_general(both, keys, transposed, preferred_element_type=F32)
         max_was = row_max[...][:, :1]
         max_now = jnp.maximum(max_was, jnp.max(scores, axis=-1, keepdims=True))
-        rescale = jnp.exp2(max_was - max_now)
-        weights = jnp.exp2(scores - max_now).astype(BF16)
+        rescale = jnp.exp(max_was - max_now)
+        weights = jnp.exp(scores - max_now).astype(BF16)
         wide = weights.astype(F32)
         shifted = wide * score_tangent
         shaded = shifted.astype(BF16)
         row_max[...] = jnp.broadcast_to(max_now, row_max.shape)
-        row_total[...] = row_total[...] * rescale + jnp.sum(wide, axis=-1, keepdims=True)
-        tilt_sum[...] = tilt_sum[...] * rescale + jnp.sum(shifted, axis=-1, keepdims=True)
+        row_total[...] = row_total[...] * rescale + by_lane(wide)
+        tilt_sum[...] = tilt_sum[...] * rescale + by_lane(shifted)
         acc[...] = acc[...] * rescale + jnp.dot(weights, vals, preferred_element_type=F32)
         acc_shaded[...] = acc_shaded[...] * rescale + jnp.dot(
             shaded, vals[:, :HD], preferred_element_type=F32
@@ -348,8 +343,7 @@
 
         piece, p = at // half, at % half
         for sub in (0, 1):
-            for part in (0, 1):
-                pair_copy(piece, p, sub, part).wait_recv()
+            pair_copy(piece, p, sub).wait_recv()
         absorb(piece, p)
         return carry
 
@@ -363,10 +357,11 @@
     ]
     for chunk in (1, 0):
         rows = slice(chunk * far_rows, (chunk + 1) * far_rows)
-        inverse = 1.0 / row_total[rows, :]
+        inverse = 1.0 / jnp.sum(row_total[rows, :], axis=-1, keepdims=True)
+        tilt = SCALE * jnp.sum(tilt_sum[rows, :], axis=-1, keepdims=True) * inverse
         attended = acc[rows, :HD] * inverse
         tangent = acc[rows, HD:] + SCALE * acc_shaded[rows, :]
-        attended_dot = tangent * inverse - (SCALE * tilt_sum[rows, :] * inverse) * attended
+        attended_dot = tangent * inverse - tilt * attended
         for at in range(nx):
             j = chunk * nx + at
             own = slice(at * tokens, (at + 1) * tokens)
@@ -382,11 +377,7 @@
     for j in range(1, group):
         out_copies[j].wait_recv()
     everything = jnp.concatenate([out_land[j] for j in range(group)], axis=1)
-    projected = jnp.dot(everything, weight[...], preferred_element_type=F32)
-    primal, dot = projected[:tokens], projected[tokens:]
-    gate, gate_dot = gates[0], gates[1]
-    out_ref[...] = (gate * primal).astype(BF16)
-    out_dot_ref[...] = (gate_dot * primal + gate * dot).astype(BF16)
+    out_ref[...] = jnp.dot(everything, weight[...], preferred_element_type=F32)
 
     for j in range(1, group):
         out_copies[j].wait_send()
@@ -398,8 +389,7 @@
     for piece in (NEAR, FAR):
         for p in range(half):
             for sub in (0, 1):
-                for part in (0, 1):
-                    pair_copy(piece, p, sub, part).wait_send()
+                pair_copy(piece, p, sub).wait_send()
 
 
 def local(
@@ -424,16 +414,14 @@
     piece_rows = nx * tokens
     half = nz // 2
     vmem = pl.BlockSpec(memory_space=pltpu.VMEM)
-    out_shape = jax.ShapeDtypeStruct((tokens, width), BF16)
     all_rows = rows * nz * 2
-    return pl.pallas_call(
+    projected = pl.pallas_call(
         functools.partial(kernel, nx, nz),
-        out_shape=(out_shape, out_shape),
-        in_specs=[pl.BlockSpec(memory_space=pl.ANY)] * 9,
-        out_specs=(vmem, vmem),
+        out_shape=jax.ShapeDtypeStruct((2 * tokens, width), F32),
+        in_specs=[pl.BlockSpec(memory_space=pl.ANY)] * 7,
+        out_specs=vmem,
         scratch_shapes=[
             pltpu.VMEM((6, tokens, group * HD), BF16),
-            pltpu.VMEM((2, 1, width), F32),
             pltpu.VMEM((2, group, 2 * tokens, HD), BF16),
             pltpu.VMEM((group, 2 * tokens, HD), BF16),
             pltpu.VMEM((2, group, 2 * tokens, HD), BF16),
@@ -451,17 +439,16 @@
             pltpu.VMEM((group, 2 * tokens, HD), BF16),
             pltpu.VMEM((group * HD, width), BF16),
             pltpu.SemaphoreType.DMA((6,)),
-            pltpu.SemaphoreType.DMA((2,)),
             pltpu.SemaphoreType.DMA((group,)),
             pltpu.SemaphoreType.DMA((2, 2, group)),
             pltpu.SemaphoreType.DMA((2, group)),
             pltpu.SemaphoreType.DMA((2, 2)),
             pltpu.SemaphoreType.DMA((2, 2)),
             pltpu.SemaphoreType.DMA((2, group)),
-            pltpu.SemaphoreType.DMA((2, 2, half, 2)),
-            pltpu.SemaphoreType.DMA((2, 2, half, 2)),
-            pltpu.SemaphoreType.DMA((2, half, 2, 2)),
-            pltpu.SemaphoreType.DMA((2, half, 2, 2)),
+            pltpu.SemaphoreType.DMA((2, 2, half, 4)),
+            pltpu.SemaphoreType.DMA((2, 2, half, 4)),
+            pltpu.SemaphoreType.DMA((2, half, 2)),
+            pltpu.SemaphoreType.DMA((2, half, 2)),
         ],
         compiler_params=pltpu.CompilerParams(
             collective_id=0, has_side_effects=True, vmem_limit_bytes=VMEM_LIMIT
@@ -479,9 +466,11 @@
         key_tangent,
         value_tangent,
         out_weight,
-        gate_vector,
-        gate_tangent,
     )
+    primal, dot = projected[:tokens], projected[tokens:]
+    block_out = (gate_vector * primal).astype(BF16)
+    block_tangent = (gate_tangent * primal + gate_vector * dot).astype(BF16)
+    return block_out, block_tangent
 
 
 def solution(mesh):

time: 80.8 us -> 79.4 us (0.983)
  the two profiles are of different devices: /device:TPU:19 before, /device:TPU:8 now
where the time goes in v4:
time: 79.4 us; the launch traced here: 79.3 us
  Pallas kernels  76.8 us (97%)
  other arithmetic  1.88 us (2%)
    pallas_call x1, Pallas kernels, local(): pl.pallas_call(functools.partial(kernel, nx, nz), out_shape=jax.ShapeDtyp...  76.8 us
    convert_element_type x1, other arithmetic, local(): block_tangent = (gate_tangent * primal + gate_vector * dot).astype(BF16)  1.88 us

profile of v4, /device:TPU:8, one launch (start us, length us, event | category | flops | bytes accessed | tf_op | source)
XLA Modules:
  0.0 79.3 jit_solution(6056467864985039446)
XLA Ops:
  0.6 76.8 %shard_map.104 = f32[112,1536]{1,0:T(8,128)} custom-call(bf16[56,1024]{1,0:T(8,128)(2,1)} %q_hbm.1, bf16[56,1024]{1,0:T(8,128)(2,1)} %k_hbm.1, bf16[56,1024]{1,0:T(8,128)(2,1)} %v_hbm.1, bf16[56,1024]{1,0:T(8,128)(2,1)} %qd_hbm.1, bf16[56,1024]{1,0:T(8,128)(2,1)} %kd_hbm.1, bf16[56,1024]{1,0:T(8,128)(2,1)} %vd_hbm.1, bf16[1024,1536]{1,0:T(8,128)(2,1)} %w_hbm.1), custom_call_target="tpu_custom_call" | custom-call | flops 4932501504 | bytes 14680064 | tf_op jit(solution)/shard_map/pallas_call | solution.py:418
  77.4 1.9 %add_convert_fusion = (bf16[56,1536]{1,0:T(8,128)(2,1)}, bf16[56,1536]{1,0:T(8,128)(2,1)}) fusion(f32[112,1536]{1,0:T(8,128)} %shard_map.104, f32[1536]{0:T(1024)} %param.17, f32[1536]{0:T(1024)} %param.16), kind=kLoop, calls=%fused_computation | loop fusion | flops 516096 | bytes 1044480 | tf_op jit(solution)/shard_map/convert_element_type | solution.py:472

commit v5 on v4

--- a/solution.py
+++ b/solution.py
@@ -42,6 +42,8 @@
     row_max,
     row_total,
     tilt_sum,
+    merge_send,
+    merge_land,
     out_send,
     out_land,
     weight,
@@ -54,12 +56,12 @@
     out_sems,
     ring_send_sems,
     ring_recv_sems,
-    pair_send_sems,
-    pair_recv_sems,
+    pair_sems,
 ):
     tokens = q_hbm.shape[0]
     group = 2 * nx
     far_rows = nx * tokens
+    rows_own = 2 * far_rows
     half = nz // 2
     dp = lax.axis_index("dp")
     seq = lax.axis_index("seq")
@@ -229,15 +231,6 @@
                         right if way == RIGHTWARD else left,
                     )
 
-    def pair_copy(piece, p, sub):
-        return remote(
-            kv.at[piece, p, :, sub],
-            kv.at[piece, p, :, 2 + sub],
-            pair_send_sems.at[piece, p, sub],
-            pair_recv_sems.at[piece, p, sub],
-            sibling,
-        )
-
     def start_piece(piece):
         members = range(piece * nx, (piece + 1) * nx)
         for copy in near_kv if piece == NEAR else far_kv[0] + far_kv[1]:
@@ -253,7 +246,6 @@
             for way in (RIGHTWARD, LEFTWARD):
                 if steps_of(piece, way) >= 1:
                     ring_copies[piece, way, 1, part].start()
-        pair_copy(piece, half - 1, 0).start()
 
     def pass_on(piece, step):
         for part in range(4):
@@ -262,15 +254,13 @@
                     ring_copies[piece, way, step, part].wait_recv()
                     if step + 1 <= steps_of(piece, way):
                         ring_copies[piece, way, step + 1, part].start()
-                    if part == 3:
-                        pair_copy(piece, *slot(way, step)).start()
 
     def gather_queries():
         for copies in [near_q] + far_q:
             for copy in copies:
                 copy.wait_recv()
         for side, at in ((0, tokens), (1, 0)):
-            q_all[:, side * HD : (side + 1) * HD] = jnp.concatenate(
+            q_all[:rows_own, side * HD : (side + 1) * HD] = jnp.concatenate(
                 [
                     (send_q if j == 0 else land_q)[j].astype(F32)[at : at + tokens]
                     for j in range(group)
@@ -278,15 +268,38 @@
                 axis=0,
             ).astype(BF16)
 
+    queries_over = remote(
+        q_all.at[pl.ds(0, rows_own)],
+        q_all.at[pl.ds(rows_own, rows_own)],
+        pair_sems.at[0, 2],
+        pair_sems.at[1, 2],
+        sibling,
+    )
+    merge_copies = [
+        remote(
+            merge_send.at[:, pl.ds(chunk * far_rows, far_rows)],
+            merge_land.at[:, pl.ds(chunk * far_rows, far_rows)],
+            pair_sems.at[0, chunk],
+            pair_sems.at[1, chunk],
+            sibling,
+        )
+        for chunk in (0, 1)
+    ]
+
     def by_lane(block):
+        width = block.shape[1]
+        whole = width - width % HD
         total = block[:, :HD]
-        for at in range(HD, block.shape[1], HD):
+        for at in range(HD, whole, HD):
             total = total + block[:, at : at + HD]
+        if width > whole:
+            empty = jnp.zeros((block.shape[0], HD - width + whole), F32)
+            total = total + jnp.concatenate([block[:, whole:], empty], axis=1)
         return total
 
     def absorb(piece, p):
-        keys = kv[piece, p, 0].reshape(4 * far_rows, 2 * HD)
-        vals = kv[piece, p, 1].reshape(4 * far_rows, 2 * HD)
+        keys = kv[piece, p, 0].reshape(2 * far_rows, 2 * HD)
+        vals = kv[piece, p, 1].reshape(2 * far_rows, 2 * HD)
         both = q_all[...]
         transposed = (((1,), (1,)), ((), ()))
         scores = lax.dot_general(
@@ -340,10 +353,10 @@
                 if now == 0:
                     start_piece(FAR)
                     gather_queries()
+                    queries_over.start()
+                    queries_over.wait_recv()
 
         piece, p = at // half, at % half
-        for sub in (0, 1):
-            pair_copy(piece, p, sub).wait_recv()
         absorb(piece, p)
         return carry
 
@@ -355,13 +368,38 @@
         else remote(out_send.at[j], out_land.at[j], out_sems.at[0, j], out_sems.at[1, j], giver(j))
         for j in range(group)
     ]
+
+    def state(first):
+        rows = slice(first, first + far_rows)
+        return (
+            acc[rows, :HD],
+            acc[rows, HD:] + SCALE * acc_shaded[rows, :],
+            row_max[rows, :][:, :1],
+            jnp.sum(row_total[rows, :], axis=-1, keepdims=True),
+            SCALE * jnp.sum(tilt_sum[rows, :], axis=-1, keepdims=True),
+        )
+
+    lane = lax.broadcasted_iota(jnp.int32, (far_rows, HD), 1)
     for chunk in (1, 0):
         rows = slice(chunk * far_rows, (chunk + 1) * far_rows)
-        inverse = 1.0 / jnp.sum(row_total[rows, :], axis=-1, keepdims=True)
-        tilt = SCALE * jnp.sum(tilt_sum[rows, :], axis=-1, keepdims=True) * inverse
-        attended = acc[rows, :HD] * inverse
-        tangent = acc[rows, HD:] + SCALE * acc_shaded[rows, :]
-        attended_dot = tangent * inverse - tilt * attended
+        weighted, tangent, top, total, tilt = state(rows_own + chunk * far_rows)
+        merge_send[0, rows, :] = weighted
+        merge_send[1, rows, :] = tangent
+        merge_send[2, rows, :] = jnp.where(lane == 0, top, jnp.where(lane == 1, total, tilt))
+        merge_copies[chunk].start()
+    for chunk in (1, 0):
+        rows = slice(chunk * far_rows, (chunk + 1) * far_rows)
+        weighted, tangent, top, total, tilt = state(chunk * far_rows)
+        merge_copies[chunk].wait_recv()
+        other = merge_land[2, rows, :]
+        other_top = other[:, 0:1]
+        joint = jnp.maximum(top, other_top)
+        mine, theirs = jnp.exp(top - joint), jnp.exp(other_top - joint)
+        inverse = 1.0 / (mine * total + theirs * other[:, 1:2])
+        mine, theirs = mine * inverse, theirs * inverse
+        attended = mine * weighted + theirs * merge_land[0, rows, :]
+        tilt = mine * tilt + theirs * other[:, 2:3]
+        attended_dot = mine * tangent + theirs * merge_land[1, rows, :] - tilt * attended
         for at in range(nx):
             j = chunk * nx + at
             own = slice(at * tokens, (at + 1) * tokens)
@@ -386,10 +424,9 @@
             copy.wait_send()
     for copy in ring_copies.values():
         copy.wait_send()
-    for piece in (NEAR, FAR):
-        for p in range(half):
-            for sub in (0, 1):
-                pair_copy(piece, p, sub).wait_send()
+    queries_over.wait_send()
+    for copy in merge_copies:
+        copy.wait_send()
 
 
 def local(
@@ -428,13 +465,15 @@
             pltpu.VMEM((group, 2 * tokens, HD), BF16),
             pltpu.VMEM((2, nx, 2 * tokens, HD), BF16),
             pltpu.VMEM((nx, 2 * tokens, HD), BF16),
-            pltpu.VMEM((2, half, 2, 4, piece_rows, 2 * HD), BF16),
-            pltpu.VMEM((rows, 2 * HD), BF16),
-            pltpu.VMEM((rows, 2 * HD), F32),
-            pltpu.VMEM((rows, HD), F32),
-            pltpu.VMEM((rows, HD), F32),
-            pltpu.VMEM((rows, HD), F32),
-            pltpu.VMEM((rows, HD), F32),
+            pltpu.VMEM((2, half, 2, 2, piece_rows, 2 * HD), BF16),
+            pltpu.VMEM((2 * rows, 2 * HD), BF16),
+            pltpu.VMEM((2 * rows, 2 * HD), F32),
+            pltpu.VMEM((2 * rows, HD), F32),
+            pltpu.VMEM((2 * rows, HD), F32),
+            pltpu.VMEM((2 * rows, HD), F32),
+            pltpu.VMEM((2 * rows, HD), F32),
+            pltpu.VMEM((3, rows, HD), F32),
+            pltpu.VMEM((3, rows, HD), F32),
             pltpu.VMEM((group, 2 * tokens, HD), BF16),
             pltpu.VMEM((group, 2 * tokens, HD), BF16),
             pltpu.VMEM((group * HD, width), BF16),
@@ -447,8 +486,7 @@
             pltpu.SemaphoreType.DMA((2, group)),
             pltpu.SemaphoreType.DMA((2, 2, half, 4)),
             pltpu.SemaphoreType.DMA((2, 2, half, 4)),
-            pltpu.SemaphoreType.DMA((2, half, 2)),
-            pltpu.SemaphoreType.DMA((2, half, 2)),
+            pltpu.SemaphoreType.DMA((2, 3)),
         ],
         compiler_params=pltpu.CompilerParams(
             collective_id=0, has_side_effects=True, vmem_limit_bytes=VMEM_LIMIT

time: 79.4 us -> 78.8 us (level)
  the two profiles are of different devices: /device:TPU:8 before, /device:TPU:9 now
where the time goes in v5:
time: 78.8 us; the launch traced here: 78.6 us
  Pallas kernels  76.1 us (97%)
  other arithmetic  1.88 us (2%)
    pallas_call x1, Pallas kernels, local(): pl.pallas_call(functools.partial(kernel, nx, nz), out_shape=jax.ShapeDtyp...  76.1 us
    convert_element_type x1, other arithmetic, local(): block_tangent = (gate_tangent * primal + gate_vector * dot).astype(BF16)  1.88 us

profile of v5, /device:TPU:9, one launch (start us, length us, event | category | flops | bytes accessed | tf_op | source)
XLA Modules:
  0.0 78.6 jit_solution(17077487414650908544)
XLA Ops:
  0.6 76.1 %shard_map.104 = f32[112,1536]{1,0:T(8,128)} custom-call(bf16[56,1024]{1,0:T(8,128)(2,1)} %q_hbm.1, bf16[56,1024]{1,0:T(8,128)(2,1)} %k_hbm.1, bf16[56,1024]{1,0:T(8,128)(2,1)} %v_hbm.1, bf16[56,1024]{1,0:T(8,128)(2,1)} %qd_hbm.1, bf16[56,1024]{1,0:T(8,128)(2,1)} %kd_hbm.1, bf16[56,1024]{1,0:T(8,128)(2,1)} %vd_hbm.1, bf16[1024,1536]{1,0:T(8,128)(2,1)} %w_hbm.1), custom_call_target="tpu_custom_call" | custom-call | flops 4932501504 | bytes 14680064 | tf_op jit(solution)/shard_map/pallas_call | solution.py:455
  76.7 1.9 %add_convert_fusion = (bf16[56,1536]{1,0:T(8,128)(2,1)}, bf16[56,1536]{1,0:T(8,128)(2,1)}) fusion(f32[112,1536]{1,0:T(8,128)} %shard_map.104, f32[1536]{0:T(1024)} %param.17, f32[1536]{0:T(1024)} %param.16), kind=kLoop, calls=%fused_computation | loop fusion | flops 516096 | bytes 1044480 | tf_op jit(solution)/shard_map/convert_element_type | solution.py:510

commit v6 on v4

--- a/solution.py
+++ b/solution.py
@@ -41,7 +41,6 @@
     acc_shaded,
     row_max,
     row_total,
-    tilt_sum,
     out_send,
     out_land,
     weight,
@@ -289,59 +288,58 @@
         vals = kv[piece, p, 1].reshape(4 * far_rows, 2 * HD)
         both = q_all[...]
         transposed = (((1,), (1,)), ((), ()))
-        scores = lax.dot_general(
+        scores = SCALE * lax.dot_general(
             both[:, HD:], keys[:, :HD], transposed, preferred_element_type=F32
-        ) * SCALE
-        score_tangent = lax.dot_general(both, keys, transposed, preferred_element_type=F32)
-        max_was = row_max[...][:, :1]
+        )
+        score_tangent = lax.dot_general(
+            both, keys, transposed, preferred_element_type=F32
+        ).astype(BF16)
+        max_was = row_max[...]
         max_now = jnp.maximum(max_was, jnp.max(scores, axis=-1, keepdims=True))
         rescale = jnp.exp(max_was - max_now)
-        weights = jnp.exp(scores - max_now).astype(BF16)
-        wide = weights.astype(F32)
-        shifted = wide * score_tangent
-        shaded = shifted.astype(BF16)
-        row_max[...] = jnp.broadcast_to(max_now, row_max.shape)
+        rescale_wide = jnp.concatenate([rescale, rescale], axis=1)
+        wide = jnp.exp(scores - jnp.concatenate([max_now] * (scores.shape[1] // HD), axis=1))
+        weights = wide.astype(BF16)
+        shaded = weights * score_tangent
+        row_max[...] = max_now
         row_total[...] = row_total[...] * rescale + by_lane(wide)
-        tilt_sum[...] = tilt_sum[...] * rescale + by_lane(shifted)
-        acc[...] = acc[...] * rescale + jnp.dot(weights, vals, preferred_element_type=F32)
-        acc_shaded[...] = acc_shaded[...] * rescale + jnp.dot(
-            shaded, vals[:, :HD], preferred_element_type=F32
+        acc[...] = acc[...] * rescale_wide + jnp.dot(
+            weights, vals, preferred_element_type=F32
+        )
+        vals_and_ones = jnp.concatenate([vals[:, :HD], jnp.ones((4 * far_rows, HD), BF16)], axis=1)
+        acc_shaded[...] = acc_shaded[...] * rescale_wide + jnp.dot(
+            shaded, vals_and_ones, preferred_element_type=F32
         )
 
     row_max[...] = jnp.full(row_max.shape, -1e30, F32)
     row_total[...] = jnp.zeros(row_total.shape, F32)
-    tilt_sum[...] = jnp.zeros(tilt_sum.shape, F32)
     acc[...] = jnp.zeros(acc.shape, F32)
     acc_shaded[...] = jnp.zeros(acc_shaded.shape, F32)
 
     start_piece(NEAR)
     relay()
 
-    before = {at: [] for at in range(2 * half)}
-    for step in range(1, min(half, 2) + 1):
-        before[0].append((NEAR, step))
-    at = 1
-    for step in range(1, half + 1):
-        if step + 2 <= half:
-            before[at].append((NEAR, step + 2))
-            at += 1
-        before[2 * half - 1 if step == half else at].append((FAR, step))
-        at += 1
+    before = {0: [(NEAR, 1)], 1: [(NEAR, 2), (FAR, 0)], 2 * half - 1: [(FAR, half)]}
+    if half == 4:
+        before |= {2: [(NEAR, 3), (FAR, 1)], 3: [(NEAR, 4)], 4: [(FAR, 2)], 5: [(FAR, 3)]}
+    else:
+        before[1].append((FAR, 1))
 
     def block(at, carry):
         for now, arrivals in before.items():
-            if not arrivals:
-                continue
 
             @pl.when(at == now)
             def _(now=now, arrivals=arrivals):
                 for piece, step in arrivals:
-                    pass_on(piece, step)
+                    if step == 0:
+                        start_piece(piece)
+                    else:
+                        pass_on(piece, step)
                 if now == 0:
-                    start_piece(FAR)
                     gather_queries()
 
-        piece, p = at // half, at % half
+        order = at + jnp.where(at == half - 1, 1, 0) - jnp.where(at == half, 1, 0)
+        piece, p = order // half, order % half
         for sub in (0, 1):
             pair_copy(piece, p, sub).wait_recv()
         absorb(piece, p)
@@ -358,9 +356,9 @@
     for chunk in (1, 0):
         rows = slice(chunk * far_rows, (chunk + 1) * far_rows)
         inverse = 1.0 / jnp.sum(row_total[rows, :], axis=-1, keepdims=True)
-        tilt = SCALE * jnp.sum(tilt_sum[rows, :], axis=-1, keepdims=True) * inverse
+        tilt = SCALE * acc_shaded[rows, HD:] * inverse
         attended = acc[rows, :HD] * inverse
-        tangent = acc[rows, HD:] + SCALE * acc_shaded[rows, :]
+        tangent = acc[rows, HD:] + SCALE * acc_shaded[rows, :HD]
         attended_dot = tangent * inverse - tilt * attended
         for at in range(nx):
             j = chunk * nx + at
@@ -431,8 +429,7 @@
             pltpu.VMEM((2, half, 2, 4, piece_rows, 2 * HD), BF16),
             pltpu.VMEM((rows, 2 * HD), BF16),
             pltpu.VMEM((rows, 2 * HD), F32),
-            pltpu.VMEM((rows, HD), F32),
-            pltpu.VMEM((rows, HD), F32),
+            pltpu.VMEM((rows, 2 * HD), F32),
             pltpu.VMEM((rows, HD), F32),
             pltpu.VMEM((rows, HD), F32),
             pltpu.VMEM((group, 2 * tokens, HD), BF16),

time: 79.4 us -> 78.7 us (level)
  the two profiles are of different devices: /device:TPU:8 before, /device:TPU:1 now
where the time goes in v6:
time: 78.7 us; the launch traced here: 78.4 us
  Pallas kernels  75.8 us (96%)
  other arithmetic  1.88 us (2%)
    pallas_call x1, Pallas kernels, local(): pl.pallas_call(functools.partial(kernel, nx, nz), out_shape=jax.ShapeDtyp...  75.8 us
    convert_element_type x1, other arithmetic, local(): block_tangent = (gate_tangent * primal + gate_vector * dot).astype(BF16)  1.88 us

profile of v6, /device:TPU:1, one launch (start us, length us, event | category | flops | bytes accessed | tf_op | source)
XLA Modules:
  0.0 78.4 jit_solution(2134536355064969553)
XLA Ops:
  0.6 75.8 %shard_map.104 = f32[112,1536]{1,0:T(8,128)} custom-call(bf16[56,1024]{1,0:T(8,128)(2,1)} %q_hbm.1, bf16[56,1024]{1,0:T(8,128)(2,1)} %k_hbm.1, bf16[56,1024]{1,0:T(8,128)(2,1)} %v_hbm.1, bf16[56,1024]{1,0:T(8,128)(2,1)} %qd_hbm.1, bf16[56,1024]{1,0:T(8,128)(2,1)} %kd_hbm.1, bf16[56,1024]{1,0:T(8,128)(2,1)} %vd_hbm.1, bf16[1024,1536]{1,0:T(8,128)(2,1)} %w_hbm.1), custom_call_target="tpu_custom_call" | custom-call | flops 4932501504 | bytes 14680064 | tf_op jit(solution)/shard_map/pallas_call | solution.py:416
  76.5 1.9 %add_convert_fusion = (bf16[56,1536]{1,0:T(8,128)(2,1)}, bf16[56,1536]{1,0:T(8,128)(2,1)}) fusion(f32[112,1536]{1,0:T(8,128)} %shard_map.104, f32[1536]{0:T(1024)} %param.17, f32[1536]{0:T(1024)} %param.16), kind=kLoop, calls=%fused_computation | loop fusion | flops 516096 | bytes 1044480 | tf_op jit(solution)/shard_map/convert_element_type | solution.py:469

commit v7 on v6

--- a/solution.py
+++ b/solution.py
@@ -43,6 +43,7 @@
     row_total,
     out_send,
     out_land,
+    out_relayed,
     weight,
     staged_sems,
     weight_sem,
@@ -51,6 +52,7 @@
     relay_kv_sems,
     relay_q_sems,
     out_sems,
+    out_leg_sems,
     ring_send_sems,
     ring_recv_sems,
     pair_send_sems,
@@ -192,7 +194,8 @@
                     for dx in range(low, high)
                 ]
             )
-    for copy in near_kv + leg_q + leg_kv + near_q:
+    far_first = sorted(range(1, nx), key=lambda j: -min(j, nx - j))
+    for copy in [near_kv[j - 1] for j in far_first] + leg_q + leg_kv + near_q:
         copy.start()
 
     def relay():
@@ -283,10 +286,11 @@
             total = total + block[:, at : at + HD]
         return total
 
-    def absorb(piece, p):
+    def absorb(piece, p, first, count):
+        rows = slice(first, first + count)
         keys = kv[piece, p, 0].reshape(4 * far_rows, 2 * HD)
         vals = kv[piece, p, 1].reshape(4 * far_rows, 2 * HD)
-        both = q_all[...]
+        both = q_all[rows, :]
         transposed = (((1,), (1,)), ((), ()))
         scores = SCALE * lax.dot_general(
             both[:, HD:], keys[:, :HD], transposed, preferred_element_type=F32
@@ -294,20 +298,20 @@
         score_tangent = lax.dot_general(
             both, keys, transposed, preferred_element_type=F32
         ).astype(BF16)
-        max_was = row_max[...]
+        max_was = row_max[rows, :]
         max_now = jnp.maximum(max_was, jnp.max(scores, axis=-1, keepdims=True))
         rescale = jnp.exp(max_was - max_now)
         rescale_wide = jnp.concatenate([rescale, rescale], axis=1)
         wide = jnp.exp(scores - jnp.concatenate([max_now] * (scores.shape[1] // HD), axis=1))
         weights = wide.astype(BF16)
         shaded = weights * score_tangent
-        row_max[...] = max_now
-        row_total[...] = row_total[...] * rescale + by_lane(wide)
-        acc[...] = acc[...] * rescale_wide + jnp.dot(
+        row_max[rows, :] = max_now
+        row_total[rows, :] = row_total[rows, :] * rescale + by_lane(wide)
+        acc[rows, :] = acc[rows, :] * rescale_wide + jnp.dot(
             weights, vals, preferred_element_type=F32
         )
         vals_and_ones = jnp.concatenate([vals[:, :HD], jnp.ones((4 * far_rows, HD), BF16)], axis=1)
-        acc_shaded[...] = acc_shaded[...] * rescale_wide + jnp.dot(
+        acc_shaded[rows, :] = acc_shaded[rows, :] * rescale_wide + jnp.dot(
             shaded, vals_and_ones, preferred_element_type=F32
         )
 
@@ -319,7 +323,7 @@
     start_piece(NEAR)
     relay()
 
-    before = {0: [(NEAR, 1)], 1: [(NEAR, 2), (FAR, 0)], 2 * half - 1: [(FAR, half)]}
+    before = {0: [(NEAR, 1)], 1: [(NEAR, 2), (FAR, 0)]}
     if half == 4:
         before |= {2: [(NEAR, 3), (FAR, 1)], 3: [(NEAR, 4)], 4: [(FAR, 2)], 5: [(FAR, 3)]}
     else:
@@ -342,18 +346,44 @@
         piece, p = order // half, order % half
         for sub in (0, 1):
             pair_copy(piece, p, sub).wait_recv()
-        absorb(piece, p)
+        absorb(piece, p, 0, 2 * far_rows)
         return carry
 
-    lax.fori_loop(0, 2 * half, block, 0)
-
-    out_copies = [
-        None
-        if j == 0
-        else remote(out_send.at[j], out_land.at[j], out_sems.at[0, j], out_sems.at[1, j], giver(j))
-        for j in range(group)
+    lax.fori_loop(0, 2 * half - 1, block, 0)
+    pass_on(FAR, half)
+    for sub in (0, 1):
+        pair_copy(FAR, half - 1, sub).wait_recv()
+
+    out_near = [
+        remote(out_send.at[j], out_land.at[j], out_sems.at[0, j], out_sems.at[1, j], giver(j))
+        for j in range(1, nx)
     ]
+    out_legs, out_onward = [], []
+    for way, (low, high) in enumerate(q_split):
+        if high > low:
+            out_legs.append(
+                remote(
+                    out_send.at[pl.ds(nx + low, high - low)],
+                    out_relayed.at[pl.ds(low, high - low)],
+                    out_leg_sems.at[0, way],
+                    out_leg_sems.at[1, way],
+                    along_y(way, 0),
+                )
+            )
+            out_onward.append(
+                [
+                    remote(
+                        out_relayed.at[dx],
+                        out_land.at[nx + dx],
+                        out_sems.at[0, nx + dx],
+                        out_sems.at[1, nx + dx],
+                        along_y(way, nx - dx),
+                    )
+                    for dx in range(low, high)
+                ]
+            )
     for chunk in (1, 0):
+        absorb(FAR, half - 1, chunk * far_rows, far_rows)
         rows = slice(chunk * far_rows, (chunk + 1) * far_rows)
         inverse = 1.0 / jnp.sum(row_total[rows, :], axis=-1, keepdims=True)
         tilt = SCALE * acc_shaded[rows, HD:] * inverse
@@ -368,18 +398,27 @@
                 out_land[j] = block
             else:
                 out_send[j] = block
-                out_copies[j].start()
+        for copy in out_legs if chunk == 1 else out_near:
+            copy.start()
+    for leg, copies in zip(out_legs, out_onward):
+        leg.wait_recv()
+        for copy in copies:
+            copy.start()
 
     for copy in weight_copies:
         copy.wait()
-    for j in range(1, group):
-        out_copies[j].wait_recv()
-    everything = jnp.concatenate([out_land[j] for j in range(group)], axis=1)
-    out_ref[...] = jnp.dot(everything, weight[...], preferred_element_type=F32)
-
-    for j in range(1, group):
-        out_copies[j].wait_send()
-    for copies in [near_kv, near_q, leg_kv, leg_q] + far_kv + far_q:
+    split = nx * HD
+    for copy in out_near:
+        copy.wait_recv()
+    near_heads = jnp.concatenate([out_land[j] for j in range(nx)], axis=1)
+    out_ref[...] = jnp.dot(near_heads, weight[:split, :], preferred_element_type=F32)
+    for copies in out_onward:
+        for copy in copies:
+            copy.wait_recv()
+    far_heads = jnp.concatenate([out_land[j] for j in range(nx, group)], axis=1)
+    out_ref[...] += jnp.dot(far_heads, weight[split:, :], preferred_element_type=F32)
+
+    for copies in [near_kv, near_q, leg_kv, leg_q, out_near, out_legs] + far_kv + far_q + out_onward:
         for copy in copies:
             copy.wait_send()
     for copy in ring_copies.values():
@@ -434,6 +473,7 @@
             pltpu.VMEM((rows, HD), F32),
             pltpu.VMEM((group, 2 * tokens, HD), BF16),
             pltpu.VMEM((group, 2 * tokens, HD), BF16),
+            pltpu.VMEM((nx, 2 * tokens, HD), BF16),
             pltpu.VMEM((group * HD, width), BF16),
             pltpu.SemaphoreType.DMA((6,)),
             pltpu.SemaphoreType.DMA((group,)),
@@ -442,6 +482,7 @@
             pltpu.SemaphoreType.DMA((2, 2)),
             pltpu.SemaphoreType.DMA((2, 2)),
             pltpu.SemaphoreType.DMA((2, group)),
+            pltpu.SemaphoreType.DMA((2, 2)),
             pltpu.SemaphoreType.DMA((2, 2, half, 4)),
             pltpu.SemaphoreType.DMA((2, 2, half, 4)),
             pltpu.SemaphoreType.DMA((2, half, 2)),

time: 78.7 us -> 79.8 us (1.014)
  no operation moved by 1% of the time
where the time goes in v7:
time: 79.8 us; the launch traced here: 78.9 us
  Pallas kernels  76.3 us (96%)
  other arithmetic  1.88 us (2%)
    pallas_call x1, Pallas kernels, local(): pl.pallas_call(functools.partial(kernel, nx, nz), out_shape=jax.ShapeDtyp...  76.3 us
    convert_element_type x1, other arithmetic, local(): block_tangent = (gate_tangent * primal + gate_vector * dot).astype(BF16)  1.88 us

profile of v7, /device:TPU:1, one launch (start us, length us, event | category | flops | bytes accessed | tf_op | source)
XLA Modules:
  0.0 78.9 jit_solution(7196433914853610685)
XLA Ops:
  0.6 76.3 %shard_map.104 = f32[112,1536]{1,0:T(8,128)} custom-call(bf16[56,1024]{1,0:T(8,128)(2,1)} %q_hbm.1, bf16[56,1024]{1,0:T(8,128)(2,1)} %k_hbm.1, bf16[56,1024]{1,0:T(8,128)(2,1)} %v_hbm.1, bf16[56,1024]{1,0:T(8,128)(2,1)} %qd_hbm.1, bf16[56,1024]{1,0:T(8,128)(2,1)} %kd_hbm.1, bf16[56,1024]{1,0:T(8,128)(2,1)} %vd_hbm.1, bf16[1024,1536]{1,0:T(8,128)(2,1)} %w_hbm.1), custom_call_target="tpu_custom_call" | custom-call | flops 4932501504 | bytes 14680064 | tf_op jit(solution)/shard_map/pallas_call | solution.py:455
  77.0 1.9 %add_convert_fusion = (bf16[56,1536]{1,0:T(8,128)(2,1)}, bf16[56,1536]{1,0:T(8,128)(2,1)}) fusion(f32[112,1536]{1,0:T(8,128)} %shard_map.104, f32[1536]{0:T(1024)} %param.17, f32[1536]{0:T(1024)} %param.16), kind=kLoop, calls=%fused_computation | loop fusion | flops 516096 | bytes 1044480 | tf_op jit(solution)/shard_map/convert_element_type | solution.py:510
